TPU v7x, 128 devices: a whole 4x4x4 slice. The times are simulated.
128 devices in a mesh: ctx: 32 (over x_hi, z, y), wt: 4 (over x_lo, core).
Axes of the slice: x: 4 (x_hi: 2, x_lo: 2; x = x_hi * 2 + x_lo), y: 4, z: 4, core: 2. Of those that a mesh axis runs over, the one named last changes fastest.
Arguments:
- inputs: float32 [8, 4096, 768], P('wt', 'ctx'), may hold values from -6 to 6
- lengths: int32 [8], P('wt'), may hold values from 512 to 4096, as said below
- attend_weight: float32 [768, 2304], P('wt'), may hold values from -0.21875 to 0.21875
- query_bias: float32 [768], P('wt'), may hold values from -3 to 3
- value_bias: float32 [768], P('wt'), may hold values from -0.13258252 to 0.13258252
- output_weight: float32 [768, 768], P('wt'), may hold values from -9.797959 to 9.797959
- output_bias: float32 [768], P('wt'), may hold values from -3 to 3
- norm_gain: float32 [768], P('wt'), may hold values from 0.25 to 1.75
- norm_shift: float32 [768], P('wt'), may hold values from -3 to 3
- expand_weight: float32 [768, 3072], P('wt'), may hold values from -0.21875 to 0.21875
- expand_bias: float32 [3072], P('wt'), may hold values from -3 to 3
- shrink_weight: float32 [3072, 768], P('wt'), may hold values from -0.21875 to 0.21875
- shrink_bias: float32 [768], P('wt'), may hold values from -3 to 3
- final_gain: float32 [768], P('wt'), may hold values from 0.25 to 1.75
- final_shift: float32 [768], P('wt'), may hold values from -3 to 3
- cotangent: float32 [8, 4096, 768], P('wt', 'ctx'), may hold values from -6 to 6
Outputs:
- result: float32 [8, 4096, 768], P('wt', 'ctx')
- input_grad: float32 [8, 4096, 768], P('wt', 'ctx')
- attend_grad: float32 [768, 2304], P('wt')
- query_bias_grad: float32 [768], P('wt')
- value_bias_grad: float32 [768], P('wt')
- output_grad: float32 [768, 768], P('wt')
- output_bias_grad: float32 [768], P('wt')
- norm_gain_grad: float32 [768], P('wt')
- norm_shift_grad: float32 [768], P('wt')
- expand_grad: float32 [768, 3072], P('wt')
- expand_bias_grad: float32 [3072], P('wt')
- shrink_grad: float32 [3072, 768], P('wt')
- shrink_bias_grad: float32 [768], P('wt')
- final_gain_grad: float32 [768], P('wt')
- final_shift_grad: float32 [768], P('wt')
Inputs may be any that keep to these rules, and one draw needn't show every extreme that they name: `lengths`: among the 2 sequences held by each index of wt, one, drawn from the seed, is valid at all 4096 positions; among the other sequences, one of the whole batch, drawn from the seed, is valid at exactly one eighth of 4096 positions.
All inputs are finite; a program needn't handle non-finite values.
Results may differ from a plain program's by a relative error of at most 0.03.
Values may be sent and summed in bfloat16 or wider, within the bound.
A program may use at most 320 MiB of HBM per device.

v0:
```python
import jax
import jax.numpy as jnp
from jax import lax
from jax.sharding import PartitionSpec as P

HEADS = 12
HEAD_DIM = 64


norm_eps = 1e-06
masked_score = -1e30


def layer_norm(values, gain_row, shift_row):
    centered = values - jnp.mean(values, axis=-1, keepdims=True)
    variance = jnp.mean(centered * centered, axis=-1, keepdims=True)
    return centered * lax.rsqrt(variance + norm_eps) * gain_row + shift_row


def norm_pullback(values, gain_row, upstream):
    _, pulled = jax.vjp(lambda inside, scaled: layer_norm(inside, scaled, 0.0), values, gain_row)
    grad_values, grad_gain = pulled(upstream)
    return (grad_values, grad_gain, jnp.sum(upstream, axis=0))


def exact_gelu(values):
    return jax.nn.gelu(values, approximate=False)


def key_valid(lengths, span_rows):
    positions = jnp.arange(span_rows, dtype=jnp.int32)
    return (positions[None, :] < lengths[:, None])[:, None, None, :]


def score_block(left_rows, right_rows):
    return jnp.einsum("bqhd,bkhd->bhqk", left_rows, right_rows, preferred_element_type=jnp.float32)


def score_grads(query_rows, grad_rows, key_rows, value_rows, logsum, row_delta, key_mask):
    soft_weights = jnp.where(
        key_mask, jnp.exp(score_block(query_rows, key_rows) - logsum[..., None]), 0.0
    )
    grad_weights = score_block(grad_rows, value_rows)
    grad_scores = (soft_weights * (grad_weights - row_delta[..., None])).astype(jnp.bfloat16)
    return (soft_weights, grad_scores)


def per_device(
    inputs,
    lengths,
    attend_weight,
    query_bias,
    value_bias,
    output_weight,
    output_bias,
    norm_gain,
    norm_shift,
    expand_weight,
    expand_bias,
    shrink_weight,
    shrink_bias,
    final_gain,
    final_shift,
    cotangent,
):
    shards = [
        member.astype(jnp.bfloat16)
        for member in (
            attend_weight,
            query_bias,
            value_bias,
            output_weight,
            output_bias,
            norm_gain,
            norm_shift,
            expand_weight,
            expand_bias,
            shrink_weight,
            shrink_bias,
            final_gain,
            final_shift,
        )
    ]
    gathered = (
        lax.all_gather(shards[0], "wt", axis=0, tiled=True),
        lax.all_gather(shards[1], "wt", axis=0, tiled=True),
        lax.all_gather(shards[2], "wt", axis=0, tiled=True),
        lax.all_gather(shards[3], "wt", axis=0, tiled=True),
        lax.all_gather(shards[4], "wt", axis=0, tiled=True),
        lax.all_gather(shards[5], "wt", axis=0, tiled=True),
        lax.all_gather(shards[6], "wt", axis=0, tiled=True),
        lax.all_gather(shards[7], "wt", axis=0, tiled=True),
        lax.all_gather(shards[8], "wt", axis=0, tiled=True),
        lax.all_gather(shards[9], "wt", axis=0, tiled=True),
        lax.all_gather(shards[10], "wt", axis=0, tiled=True),
        lax.all_gather(shards[11], "wt", axis=0, tiled=True),
        lax.all_gather(shards[12], "wt", axis=0, tiled=True),
    )
    params = [member.astype(jnp.float32) if member.ndim == 1 else member for member in gathered]
    (
        attend_full,
        query_add,
        value_add,
        output_full,
        output_add,
        gain_one,
        shift_one,
        expand_full,
        expand_add,
        shrink_full,
        shrink_add,
        gain_two,
        shift_two,
    ) = params
    seq_count, tok_local, model_width = inputs.shape
    row_count = seq_count * tok_local
    query_scale = HEAD_DIM ** (-0.5)
    head_shape = (seq_count, tok_local, HEADS, HEAD_DIM)
    tokens = inputs.reshape(row_count, model_width)
    tokens_low = tokens.astype(jnp.bfloat16)
    column_scale = jnp.concatenate(
        [
            jnp.full((model_width,), query_scale, jnp.float32),
            jnp.ones((2 * model_width,), jnp.float32),
        ]
    )
    bias_row = jnp.concatenate([query_add, jnp.zeros_like(query_add), value_add])
    packed = (
        (jnp.dot(tokens_low, attend_full, preferred_element_type=jnp.float32) + bias_row)
        * column_scale
    ).astype(jnp.bfloat16)
    query_rows = packed[:, :model_width].reshape(head_shape)
    key_rows = packed[:, model_width : 2 * model_width].reshape(head_shape)
    value_rows = packed[:, 2 * model_width :].reshape(head_shape)
    stat_shape = (seq_count, HEADS, tok_local)
    run_peak = jnp.full(stat_shape, masked_score, jnp.float32)
    remote_keys = lax.all_gather(key_rows, "ctx", axis=1, tiled=True)
    remote_values = lax.all_gather(value_rows, "ctx", axis=1, tiled=True)
    key_mask = key_valid(lengths, remote_keys.shape[1])
    scores = jnp.where(key_mask, score_block(query_rows, remote_keys), masked_score)
    new_peak = jnp.maximum(run_peak, jnp.max(scores, axis=-1))
    soft_weights = jnp.where(key_mask, jnp.exp(scores - new_peak[..., None]), 0.0)
    update = jnp.einsum(
        "bhqk,bkhd->bqhd",
        soft_weights.astype(jnp.bfloat16),
        remote_values,
        preferred_element_type=jnp.float32,
    )
    run_mixed = update
    run_peak, run_total, run_mixed = (new_peak, jnp.sum(soft_weights, axis=-1), run_mixed)
    logsum = run_peak + jnp.log(run_total)
    mixed = run_mixed / jnp.transpose(run_total, (0, 2, 1))[..., None]
    mixed_low = mixed.reshape(row_count, model_width).astype(jnp.bfloat16)
    attended = jnp.dot(mixed_low, output_full, preferred_element_type=jnp.float32) + output_add
    hidden_one = tokens + attended
    normed_one = layer_norm(hidden_one, gain_one, shift_one)
    normed_low = normed_one.astype(jnp.bfloat16)
    raised = jnp.dot(normed_low, expand_full, preferred_element_type=jnp.float32) + expand_add
    activated = exact_gelu(raised).astype(jnp.bfloat16)
    branch = jnp.dot(activated, shrink_full, preferred_element_type=jnp.float32) + shrink_add
    hidden_two = normed_one + branch
    result = layer_norm(hidden_two, gain_two, shift_two)
    regathered = (
        lax.all_gather(shards[0], "wt", axis=0, tiled=True),
        lax.all_gather(shards[3], "wt", axis=0, tiled=True),
        lax.all_gather(shards[5], "wt", axis=0, tiled=True),
        lax.all_gather(shards[7], "wt", axis=0, tiled=True),
        lax.all_gather(shards[9], "wt", axis=0, tiled=True),
        lax.all_gather(shards[11], "wt", axis=0, tiled=True),
    )
    attend_back, output_back, gain_back, expand_back, shrink_back, final_back = regathered
    gain_back = gain_back.astype(jnp.float32)
    final_back = final_back.astype(jnp.float32)
    upstream = cotangent.reshape(row_count, model_width)
    grad_two, final_gain_term, final_shift_term = norm_pullback(hidden_two, final_back, upstream)
    branch_low = grad_two.astype(jnp.bfloat16)
    shrink_bias_term = jnp.sum(branch_low.astype(jnp.float32), axis=0)
    shrink_term = jnp.dot(activated.T, branch_low, preferred_element_type=jnp.float32)
    grad_active = jnp.dot(branch_low, shrink_back.T, preferred_element_type=jnp.float32)
    _, gelu_pull = jax.vjp(exact_gelu, raised)
    raised_low = gelu_pull(grad_active)[0].astype(jnp.bfloat16)
    expand_bias_term = jnp.sum(raised_low.astype(jnp.float32), axis=0)
    expand_term = jnp.dot(normed_low.T, raised_low, preferred_element_type=jnp.float32)
    grad_normed = grad_two + jnp.dot(raised_low, expand_back.T, preferred_element_type=jnp.float32)
    grad_one, norm_gain_term, norm_shift_term = norm_pullback(hidden_one, gain_back, grad_normed)
    attended_low = grad_one.astype(jnp.bfloat16)
    output_bias_term = jnp.sum(attended_low.astype(jnp.float32), axis=0)
    output_term = jnp.dot(mixed_low.T, attended_low, preferred_element_type=jnp.float32)
    grad_mixed = jnp.dot(attended_low, output_back.T, preferred_element_type=jnp.float32)
    grad_mixed = grad_mixed.astype(jnp.bfloat16).reshape(head_shape)
    row_delta = jnp.sum(grad_mixed.astype(jnp.float32) * mixed, axis=-1)
    delta_heads = jnp.transpose(row_delta, (0, 2, 1))
    remote_keys = lax.all_gather(key_rows, "ctx", axis=1, tiled=True)
    remote_values = lax.all_gather(value_rows, "ctx", axis=1, tiled=True)
    key_mask = key_valid(lengths, remote_keys.shape[1])
    soft_weights, grad_scores = score_grads(
        query_rows, grad_mixed, remote_keys, remote_values, logsum, delta_heads, key_mask
    )
    grad_query = jnp.einsum(
        "bhqk,bkhd->bqhd", grad_scores, remote_keys, preferred_element_type=jnp.float32
    )
    key_part = jnp.einsum(
        "bhqk,bqhd->bkhd", grad_scores, query_rows, preferred_element_type=jnp.float32
    )
    value_part = jnp.einsum(
        "bhqk,bqhd->bkhd",
        soft_weights.astype(jnp.bfloat16),
        grad_mixed,
        preferred_element_type=jnp.float32,
    )
    grad_query, grad_keys, grad_values = (grad_query, key_part, value_part)
    summed_keys, summed_values = (
        lax.psum_scatter(
            grad_keys.astype(jnp.bfloat16), "ctx", scatter_dimension=1, tiled=True
        ).astype(jnp.float32),
        lax.psum_scatter(
            grad_values.astype(jnp.bfloat16), "ctx", scatter_dimension=1, tiled=True
        ).astype(jnp.float32),
    )
    query_part = grad_query.astype(jnp.bfloat16).reshape(row_count, model_width) * query_scale
    grad_packed = jnp.concatenate(
        [
            query_part,
            summed_keys.astype(jnp.bfloat16).reshape(row_count, model_width),
            summed_values.astype(jnp.bfloat16).reshape(row_count, model_width),
        ],
        axis=1,
    )
    attend_term = jnp.dot(tokens_low.T, grad_packed, preferred_element_type=jnp.float32)
    query_bias_term = jnp.sum(grad_packed[:, :model_width].astype(jnp.float32), axis=0)
    value_bias_term = jnp.sum(grad_packed[:, 2 * model_width :].astype(jnp.float32), axis=0)
    input_grad = grad_one + jnp.dot(grad_packed, attend_back.T, preferred_element_type=jnp.float32)
    shard_terms = (
        lax.psum_scatter(
            attend_term.astype(jnp.bfloat16), "wt", scatter_dimension=0, tiled=True
        ).astype(jnp.float32),
        lax.psum_scatter(
            query_bias_term.astype(jnp.bfloat16), "wt", scatter_dimension=0, tiled=True
        ).astype(jnp.float32),
        lax.psum_scatter(
            value_bias_term.astype(jnp.bfloat16), "wt", scatter_dimension=0, tiled=True
        ).astype(jnp.float32),
        lax.psum_scatter(
            output_term.astype(jnp.bfloat16), "wt", scatter_dimension=0, tiled=True
        ).astype(jnp.float32),
        lax.psum_scatter(
            output_bias_term.astype(jnp.bfloat16), "wt", scatter_dimension=0, tiled=True
        ).astype(jnp.float32),
        lax.psum_scatter(
            norm_gain_term.astype(jnp.bfloat16), "wt", scatter_dimension=0, tiled=True
        ).astype(jnp.float32),
        lax.psum_scatter(
            norm_shift_term.astype(jnp.bfloat16), "wt", scatter_dimension=0, tiled=True
        ).astype(jnp.float32),
        lax.psum_scatter(
            expand_term.astype(jnp.bfloat16), "wt", scatter_dimension=0, tiled=True
        ).astype(jnp.float32),
        lax.psum_scatter(
            expand_bias_term.astype(jnp.bfloat16), "wt", scatter_dimension=0, tiled=True
        ).astype(jnp.float32),
        lax.psum_scatter(
            shrink_term.astype(jnp.bfloat16), "wt", scatter_dimension=0, tiled=True
        ).astype(jnp.float32),
        lax.psum_scatter(
            shrink_bias_term.astype(jnp.bfloat16), "wt", scatter_dimension=0, tiled=True
        ).astype(jnp.float32),
        lax.psum_scatter(
            final_gain_term.astype(jnp.bfloat16), "wt", scatter_dimension=0, tiled=True
        ).astype(jnp.float32),
        lax.psum_scatter(
            final_shift_term.astype(jnp.bfloat16), "wt", scatter_dimension=0, tiled=True
        ).astype(jnp.float32),
    )
    (
        attend_part,
        query_bias_part,
        value_bias_part,
        output_part,
        output_bias_part,
        norm_gain_part,
        norm_shift_part,
        expand_part,
        expand_bias_part,
        shrink_part,
        shrink_bias_part,
        final_gain_part,
        final_shift_part,
    ) = shard_terms
    summed = (
        lax.psum(attend_part.astype(jnp.bfloat16), "ctx").astype(jnp.float32),
        lax.psum(query_bias_part.astype(jnp.bfloat16), "ctx").astype(jnp.float32),
        lax.psum(value_bias_part.astype(jnp.bfloat16), "ctx").astype(jnp.float32),
        lax.psum(output_part.astype(jnp.bfloat16), "ctx").astype(jnp.float32),
        lax.psum(output_bias_part.astype(jnp.bfloat16), "ctx").astype(jnp.float32),
        lax.psum(norm_gain_part.astype(jnp.bfloat16), "ctx").astype(jnp.float32),
        lax.psum(norm_shift_part.astype(jnp.bfloat16), "ctx").astype(jnp.float32),
        lax.psum(expand_part.astype(jnp.bfloat16), "ctx").astype(jnp.float32),
        lax.psum(expand_bias_part.astype(jnp.bfloat16), "ctx").astype(jnp.float32),
        lax.psum(shrink_part.astype(jnp.bfloat16), "ctx").astype(jnp.float32),
        lax.psum(shrink_bias_part.astype(jnp.bfloat16), "ctx").astype(jnp.float32),
        lax.psum(final_gain_part.astype(jnp.bfloat16), "ctx").astype(jnp.float32),
        lax.psum(final_shift_part.astype(jnp.bfloat16), "ctx").astype(jnp.float32),
    )
    return (
        result.reshape(inputs.shape),
        input_grad.reshape(inputs.shape),
        summed[0],
        summed[1],
        summed[2],
        summed[3],
        summed[4],
        summed[5],
        summed[6],
        summed[7],
        summed[8],
        summed[9],
        summed[10],
        summed[11],
        summed[12],
    )


def solution(mesh):
    placed = (
        P("wt", "ctx", None),
        P("wt"),
        P("wt", None),
        P("wt"),
        P("wt"),
        P("wt", None),
        P("wt"),
        P("wt"),
        P("wt"),
        P("wt", None),
        P("wt"),
        P("wt", None),
        P("wt"),
        P("wt"),
        P("wt"),
        P("wt", "ctx", None),
    )
    return jax.shard_map(
        per_device,
        mesh=mesh,
        in_specs=placed,
        out_specs=(
            P("wt", "ctx", None),
            P("wt", "ctx", None),
            P("wt", None),
            P("wt"),
            P("wt"),
            P("wt", None),
            P("wt"),
            P("wt"),
            P("wt"),
            P("wt", None),
            P("wt"),
            P("wt", None),
            P("wt"),
            P("wt"),
            P("wt"),
        ),
        check_vma=False,
    )
```

profile of v0, /device:TPU:0, one launch (start us, length us, event | category | flops | bytes accessed | tf_op | source)
XLA Modules:
  0.0 1740.0 jit_solution(12634978769734045465)
XLA Ops:
  7.3 2.6 convert_element_type.233
  12.9 11.3 all-reduce.20
  24.3 29.2 %all-gather.8.cloned.1.call-done = bf16[768,2304]{1,0:T(8,128)(2,1)} async-done(((bf16[192,2304]{1,0:T(8,128)(2,1)}), bf16[768,2304]{1,0:T(8,128)(2,1)}) %all-gather.8.cloned.1.call-update) | async-done | bytes 3538960 | tf_op jit(solution)/shard_map/all_gather | solution.py:85
  53.5 3.1 fusion.15
  57.0 0.8 copy.56
  58.2 0.8 copy.53
  59.1 0.7 convert_element_type.242
  59.9 2.8 convert_element_type.250
  62.8 2.8 convert_element_type.254
  68.7 5.2 all-gather
  74.9 154.1 %all-gather.12.cloned.1.call-done = bf16[2,4096,12,64]{1,3,2,0:T(8,128)(2,1)} async-done(((bf16[2,128,12,64]{1,3,2,0:T(8,128)(2,1)}), bf16[2,4096,12,64]{1,3,2,0:T(8,128)(2,1)}) %all-gather.12.cloned.1.call-update) | async-done | bytes 12582928 | tf_op jit(solution)/shard_map/all_gather | solution.py:137
  229.0 22.8 %select_reduce_fusion = (f32[2,12,128]{2,1,0:T(8,128)S(1)}, f32[2,12,128,4096]{3,2,1,0:T(8,128)}) fusion(pred[2,4096]{1,0:T(4,128)(4,1)S(1)} %iota_compare_fusion, bf16[2,4096,12,64]{1,3,2,0:T(8,128)(2,1)} %all-gather.12.cloned.1.call-done, bf16[2,128,12,64]{1,0,3,2:T(2,128)(2,1)S(1)} %reshape.159), kind=kOutput, calls=%fused_computation.3 | convolution fusion | flops 1635775488 | bytes 63328256 | tf_op jit(solution)/shard_map/bqhd,bkhd->bhqk/dot_general | solution.py:36
  251.7 22.1 %fusion.1 = f32[2,12,128]{2,1,0:T(8,128)S(1)} fusion(f32[2,12,128,4096]{3,2,1,0:T(8,128)} %get-tuple-element.113, f32[2,12,128]{2,1,0:T(8,128)S(1)} %broadcast_maximum_fusion, pred[2,4096]{1,0:T(4,128)(4,1)S(1)} %iota_compare_fusion), kind=kLoop, calls=%fused_computation.5 | loop fusion | flops 50328576 | bytes 50364416 | tf_op jit(solution)/shard_map/reduce_sum | solution.py:150
  273.9 125.8 %all-gather.10.cloned.1.call-done = bf16[2,4096,12,64]{1,3,2,0:T(8,128)(2,1)} async-done(((bf16[2,128,12,64]{1,3,2,0:T(8,128)(2,1)}), bf16[2,4096,12,64]{1,3,2,0:T(8,128)(2,1)}) %all-gather.10.cloned.1.call-update) | async-done | bytes 12582928 | tf_op jit(solution)/shard_map/all_gather | solution.py:138
  399.7 22.9 %fusion.57 = (bf16[2,128,12,64]{1,3,2,0:T(8,128)(2,1)S(1)}, f32[2,128,12,64]{1,3,2,0:T(8,128)S(1)}) fusion(f32[2,128,12]{1,2,0:T(8,128)S(1)} %bitcast.114, bf16[2,4096,12,64]{1,3,2,0:T(8,128)(2,1)} %all-gather.10.cloned.1.call-done, f32[2,12,128,4096]{3,2,1,0:T(8,128)} %get-tuple-element.113, f32[2,12,128]{2,1,0:T(8,128)S(1)} %broadcast_maximum_fusion, ...), kind=kOutput, calls=%fused_computation.106 | convolution fusion | flops 1661337600 | bytes 64126976 | tf_op jit(solution)/shard_map/bhqk,bkhd->bqhd/dot_general | solution.py:143
  423.1 2.0 fusion.58
  425.9 1.3 log_add_fusion
  427.2 47.3 %all-gather.16.cloned.1.call-done = bf16[768,3072]{1,0:T(8,128)(2,1)} async-done(((bf16[192,3072]{1,0:T(8,128)(2,1)}), bf16[768,3072]{1,0:T(8,128)(2,1)}) %all-gather.16.cloned.1.call-update) | async-done | bytes 4718608 | tf_op jit(solution)/shard_map/all_gather | solution.py:92
  474.5 11.5 multiply_convert_fusion.1
  486.1 42.3 %all-gather.18.cloned.1.call-done = bf16[3072,768]{1,0:T(8,128)(2,1)} async-done(((bf16[768,768]{1,0:T(8,128)(2,1)}), bf16[3072,768]{1,0:T(8,128)(2,1)}) %all-gather.18.cloned.1.call-update) | async-done | bytes 4718608 | tf_op jit(solution)/shard_map/all_gather | solution.py:94
  528.4 4.0 fusion.59
  532.7 0.9 fusion.31
  534.8 2.7 fusion.50
  537.6 2.2 multiply_reduce_fusion
  540.2 0.8 fusion.51
  541.1 0.7 copy-done.13
  542.7 30.7 %multiply_convert_fusion = bf16[2,12,128,4096]{3,2,1,0:T(8,128)(2,1)} fusion(f32[2,12,128,4096]{3,2,1,0:T(8,128)} %get-tuple-element.113, f32[2,12,128]{2,1,0:T(8,128)S(1)} %bitcast.113, f32[2,12,128]{2,1,0:T(8,128)S(1)} %copy-done.26, pred[2,4096]{1,0:T(4,128)(4,1)S(1)} %iota_compare_fusion, bf16[2,4096,12,64]{1,3,2,0:T(8,128)(2,1)} %all-gather.10.cloned.1.call-done, ...), kind=kOutput, calls=%fused_computation | convolution fusion | flops 1673527296 | bytes 88506368 | tf_op jit(solution)/shard_map/bqhd,bkhd->bhqk/dot_general | solution.py:36
  573.4 14.7 convert_bitcast_fusion.1
  588.1 45.2 %copy.68 = bf16[2,4096,12,64]{3,2,0,1:T(8,128)(2,1)} copy(bf16[2,4096,12,64]{1,3,2,0:T(8,128)(2,1)} %convert_bitcast_fusion.1) | data formatting | bytes 25165824
  633.4 41.7 %reshape.210 = bf16[4096,1536]{1,0:T(8,128)(2,1)} reshape(bf16[4096,2,12,64]{3,2,1,0:T(8,128)(2,1)} %bitcast.101) | data formatting | bytes 25165824
  675.1 23.9 %convert_bitcast_fusion = bf16[2,4096,12,64]{1,3,2,0:T(8,128)(2,1)} fusion(f32[2,12,128,4096]{3,2,1,0:T(8,128)} %get-tuple-element.113, f32[2,12,128]{2,1,0:T(8,128)S(1)} %copy-done.26, pred[2,4096]{1,0:T(4,128)(4,1)S(1)} %iota_compare_fusion, bf16[2,128,12,64]{1,0,3,2:T(2,128)(2,1)S(1)} %reshape.163), kind=kOutput, calls=%fused_computation.13 | convolution fusion | flops 1654652928 | bytes 63328256 | tf_op jit(solution)/shard_map/bhqk,bqhd->bkhd/dot_general | solution.py:205
  699.0 45.3 %copy.70 = bf16[2,4096,12,64]{3,2,0,1:T(8,128)(2,1)} copy(bf16[2,4096,12,64]{1,3,2,0:T(8,128)(2,1)} %convert_bitcast_fusion) | data formatting | bytes 25165824
  744.2 42.0 %reshape.212 = bf16[4096,1536]{1,0:T(8,128)(2,1)} reshape(bf16[4096,2,12,64]{3,2,1,0:T(8,128)(2,1)} %bitcast.102) | data formatting | bytes 25165824
  786.3 16.6 fusion.60
  803.3 0.8 bitcast_dynamic-update-slice_fusion.2
  804.1 122.4 %reduce-scatter.19.cloned.1.call-done = bf16[128,1536]{1,0:T(8,128)(2,1)} async-done(((bf16[4096,1536]{1,0:T(8,128)(2,1)}), bf16[128,1536]{1,0:T(8,128)(2,1)}) %reduce-scatter.19.cloned.1.call-update) | async-done | bytes 393232
  926.5 1.8 reshape.211
  928.3 1.3 copy.64
  929.6 249.2 %reduce-scatter.21.cloned.1.call-done = bf16[128,1536]{1,0:T(8,128)(2,1)} async-done(((bf16[4096,1536]{1,0:T(8,128)(2,1)}), bf16[128,1536]{1,0:T(8,128)(2,1)}) %reduce-scatter.21.cloned.1.call-update) | async-done | bytes 393232
  1178.9 1.8 reshape.213
  1180.7 1.3 copy.66
  1182.1 0.8 bitcast_dynamic-update-slice_fusion.1
  1182.9 0.8 bitcast_dynamic-update-slice_fusion
  1183.7 2.4 fusion.13
  1186.1 4.1 copy.72
  1190.3 0.9 copy-done.12
  1191.3 1.5 convolution_convert_fusion.3
  1192.9 3.8 convolution_convert_fusion.1
  1196.8 1.3 copy-done.10
  1198.2 3.6 convolution_convert_fusion
  1202.0 25.2 %reduce-scatter.23.cloned.1.call-done = bf16[192,2304]{1,0:T(8,128)(2,1)} async-done(((bf16[768,2304]{1,0:T(8,128)(2,1)}), bf16[192,2304]{1,0:T(8,128)(2,1)}) %reduce-scatter.23.cloned.1.call-update) | async-done | bytes 884752
  1227.2 2.3 copy.73
  1229.6 21.4 %reduce-scatter.13.cloned.1.call-done = bf16[192,768]{1,0:T(8,128)(2,1)} async-done(((bf16[768,768]{1,0:T(8,128)(2,1)}), bf16[192,768]{1,0:T(8,128)(2,1)}) %reduce-scatter.13.cloned.1.call-update) | async-done | bytes 294928 | tf_op jit(solution)/shard_map/reduce_scatter | solution.py:243
  1251.0 53.1 %reduce-scatter.15.cloned.1.call-done = bf16[192,3072]{1,0:T(8,128)(2,1)} async-done(((bf16[768,3072]{1,0:T(8,128)(2,1)}), bf16[192,3072]{1,0:T(8,128)(2,1)}) %reduce-scatter.15.cloned.1.call-update) | async-done | bytes 1179664 | tf_op jit(solution)/shard_map/reduce_scatter | solution.py:255
  1304.1 52.9 %reduce-scatter.17.cloned.1.call-done = bf16[768,768]{1,0:T(8,128)(2,1)} async-done(((bf16[3072,768]{1,0:T(8,128)(2,1)}), bf16[768,768]{1,0:T(8,128)(2,1)}) %reduce-scatter.17.cloned.1.call-update) | async-done | bytes 1179664 | tf_op jit(solution)/shard_map/reduce_scatter | solution.py:261
  1359.3 10.3 all-reduce.19
  1370.2 97.8 %all-reduce.17 = (bf16[192]{0:T(256)(128)(2,1)S(1)}, bf16[192]{0:T(256)(128)(2,1)S(1)}, bf16[192]{0:T(256)(128)(2,1)S(1)}, bf16[192]{0:T(256)(128)(2,1)S(1)}, bf...) all-reduce(bf16[192]{0:T(256)(128)(2,1)S(1)} %dynamic-slice.9, ...), channel_id=1, replica_groups=mesh['ctx'=32,'wt'=4] {'ctx'}, use_global_device_ids=true, to_apply=%region_17.18 | all-reduce | flops 2304 | bytes 9216 | tf_op jit(solution)/shard_map/psum | solution.py:291
  1473.2 1.1 multiply_add_fusion
  1474.3 4.4 convolution_add_fusion.3
  1478.7 247.6 %all-reduce.23.cloned.1.call-done = (bf16[192,2304]{0,1:T(8,128)(2,1)}, bf16[192,768]{1,0:T(8,128)(2,1)}, bf16[192,3072]{1,0:T(8,128)(2,1)}, bf16[768,768]{1,0:T(8,128)(2,1)}) async-done(((bf16[192,2304]{0,1:T(8,128)(2,1)}, bf16[192,768]{1,0:T(8,128)(2,1)}, bf16[192,3072]{1,0:T(8,128)(2,1)}, bf16[768,768]{1,0:T(8,128)(2,1)}), (bf16[192,2304]{0,1:T(8,128)(2,1)}, bf16[192,768]{1,0:T(8,128)(2,1)}, ...) | async-done | bytes 3538960 | tf_op jit(solution)/shard_map/psum | solution.py:290
  1726.3 2.6 copy.67
  1728.9 0.9 convert_element_type.279
  1729.8 1.7 convert_element_type.286
  1731.5 1.6 convert_element_type.289
  (261 shorter events, 18.8 us)
Async XLA Ops:
  7.2 3.0 copy-start.56
  7.2 46.3 %copy-start.66 = (f32[2304]{0:T(1024)S(1)}, f32[2304]{0:T(1024)}, u32[]{:S(2)}) copy-start(f32[2304]{0:T(1024)} %constant.40.clone.1) | copy-start | bytes 27652
  7.2 2.8 copy-start.58
  7.2 2.8 copy-start.59
  7.2 2.8 copy-start.60
  7.2 2.8 copy-start.61
  7.2 2.8 copy-start.62
  7.3 2.8 copy-start.63
  7.3 2.8 copy-start.64
  7.3 16.9 copy-start.15
  7.3 46.2 %all-gather.8.cloned.1.call-start = ((), (), s32[]{:S(2)}) async-start(), calls=%async_computation.6 | async-start | bytes 4423680 | tf_op jit(solution)/shard_map/all_gather | solution.py:85
  9.9 219.0 %all-gather.12.cloned.1.call-start = ((), (), s32[]{:S(2)}) async-start(), calls=%async_computation.8 | async-start | bytes 12976128 | tf_op jit(solution)/shard_map/all_gather | solution.py:137
  24.2 32.4 %copy-start.18 = (bf16[256,768]{1,0:T(8,128)(2,1)}, bf16[256,768]{1,0:T(8,128)(2,1)S(1)}, u32[]{:S(2)}) copy-start(bf16[256,768]{1,0:T(8,128)(2,1)S(1)} %bitcast_convert_fusion) | copy-start | bytes 1179652
  57.8 341.8 %all-gather.10.cloned.1.call-start = ((), (), s32[]{:S(2)}) async-start(), calls=%async_computation.7 | async-start | bytes 12976128 | tf_op jit(solution)/shard_map/all_gather | solution.py:138
  59.0 364.0 %all-gather.14.cloned.1.call-start = ((), (), s32[]{:S(2)}) async-start(), calls=%async_computation.9 | async-start | bytes 1474560 | tf_op jit(solution)/shard_map/all_gather | solution.py:88
  59.9 414.6 %all-gather.16.cloned.1.call-start = ((), (), s32[]{:S(2)}) async-start(), calls=%async_computation.10 | async-start | bytes 5898240 | tf_op jit(solution)/shard_map/all_gather | solution.py:92
  62.8 3.0 copy-start.51
  62.8 11.8 copy-start.57
  62.8 465.6 %all-gather.18.cloned.1.call-start = ((), (), s32[]{:S(2)}) async-start(), calls=%async_computation.11 | async-start | bytes 5898240 | tf_op jit(solution)/shard_map/all_gather | solution.py:94
  65.7 860.8 %reduce-scatter.19.cloned.1.call-start = ((), (), s32[]{:S(2)}) async-start(), calls=%async_computation.15 | async-start | bytes 12976128
  251.7 22.1 %copy-start.30 = (f32[2,12,128]{2,1,0:T(8,128)}, f32[2,12,128]{2,1,0:T(8,128)S(1)}, u32[]{:S(2)}) copy-start(f32[2,12,128]{2,1,0:T(8,128)S(1)} %get-tuple-element.112) | copy-start | bytes 36868
  273.8 148.7 %copy-start.32 = (f32[2,12,128]{2,1,0:T(8,128)}, f32[2,12,128]{2,1,0:T(8,128)S(1)}, u32[]{:S(2)}) copy-start(f32[2,12,128]{2,1,0:T(8,128)S(1)} %fusion.1) | copy-start | bytes 36868
  423.0 51.5 %copy-start.11 = (bf16[2,128,12,64]{1,0,3,2:T(2,128)(2,1)}, bf16[2,128,12,64]{1,0,3,2:T(2,128)(2,1)S(1)}, u32[]{:S(2)}) copy-start(bf16[2,128,12,64]{1,0,3,2:T(2,128)(2,1)S(1)} %copy.58) | copy-start | bytes 1179652
  423.0 2.9 copy-start.33
  425.0 114.8 %copy-start = (f32[256,768]{1,0:T(8,128)}, f32[256,768]{1,0:T(8,128)S(1)}, u32[]{:S(2)}) copy-start(f32[256,768]{1,0:T(8,128)S(1)} %get-tuple-element.117) | copy-start | bytes 2359300
  425.1 49.5 %copy-start.38 = (f32[256]{0:T(256)}, f32[256]{0:T(256)S(1)}, u32[]{:S(2)}) copy-start(f32[256]{0:T(256)S(1)} %broadcast_multiply_fusion.1) | copy-start | bytes 3076
  425.3 49.2 %copy-start.45 = (f32[256]{0:T(256)}, f32[256]{0:T(256)S(1)}, u32[]{:S(2)}) copy-start(f32[256]{0:T(256)S(1)} %multiply_reduce_fusion.5) | copy-start | bytes 3076
  486.0 46.3 %copy-start.9 = (bf16[256,3072]{1,0:T(8,128)(2,1)}, bf16[256,3072]{1,0:T(8,128)(2,1)S(1)}, u32[]{:S(2)}) copy-start(bf16[256,3072]{1,0:T(8,128)(2,1)S(1)} %get-tuple-element.105) | copy-start | bytes 4718596
  528.4 6.3 slice-start.2
  528.4 4.3 copy-start.6
  528.4 4.3 copy-start.34
  528.4 6.3 slice-start.3
  528.4 6.3 copy-start.68
  534.0 3.6 slice-start
  534.7 2.8 copy-start.19
  534.8 2.8 copy-start.28
  534.8 2.8 copy-start.39
  534.8 2.8 copy-start.43
  534.8 2.8 slice-start.1
  540.2 33.2 %copy-start.16 = (f32[256,768]{1,0:T(8,128)}, f32[256,768]{1,0:T(8,128)S(1)}, u32[]{:S(2)}) copy-start(f32[256,768]{1,0:T(8,128)S(1)} %get-tuple-element.102) | copy-start | bytes 2359300
  540.2 33.2 %copy-start.52 = (f32[256]{0:T(256)}, f32[256]{0:T(256)S(1)}, u32[]{:S(2)}) copy-start(f32[256]{0:T(256)S(1)} %negate_multiply_fusion.1) | copy-start | bytes 3076
  675.1 503.8 %reduce-scatter.21.cloned.1.call-start = ((), (), s32[]{:S(2)}) async-start(), calls=%async_computation.16 | async-start | bytes 12976128
  786.2 440.9 %reduce-scatter.23.cloned.1.call-start = ((), (), s32[]{:S(2)}) async-start(), calls=%async_computation.17 | async-start | bytes 4423680
  1190.3 60.8 %reduce-scatter.13.cloned.1.call-start = ((), (), s32[]{:S(2)}) async-start(), calls=%async_computation.12 | async-start | bytes 1474560 | tf_op jit(solution)/shard_map/reduce_scatter | solution.py:243
  1192.8 111.3 %reduce-scatter.15.cloned.1.call-start = ((), (), s32[]{:S(2)}) async-start(), calls=%async_computation.13 | async-start | bytes 5898240 | tf_op jit(solution)/shard_map/reduce_scatter | solution.py:255
  1196.8 160.2 %reduce-scatter.17.cloned.1.call-start = ((), (), s32[]{:S(2)}) async-start(), calls=%async_computation.14 | async-start | bytes 5898240 | tf_op jit(solution)/shard_map/reduce_scatter | solution.py:261
  1201.9 155.2 %copy-start.7 = (f32[2,128,768]{2,1,0:T(8,128)S(1)}, f32[2,128,768]{2,1,0:T(8,128)}, u32[]{:S(2)}) copy-start(f32[2,128,768]{2,1,0:T(8,128)} %param.31) | copy-start | bytes 2359300
  1201.9 156.6 %copy-start.65 = (f32[192]{0:T(256)S(1)}, f32[192]{0:T(256)}, u32[]{:S(2)}) copy-start(f32[192]{0:T(256)} %param.30) | copy-start | bytes 2308
  1201.9 157.0 %copy-start.5 = (bf16[128,2,12,64]{3,2,1,0:T(8,128)(2,1)S(1)}, bf16[128,2,12,64]{3,2,1,0:T(8,128)(2,1)}, u32[]{:S(2)}) copy-start(bf16[128,2,12,64]{3,2,1,0:T(8,128)(2,1)} %copy-done.4) | copy-start | bytes 1179652
  1201.9 524.4 %all-reduce.23.cloned.1.call-start = ((), (), s32[]{:S(2)}) async-start(), calls=%async_computation.18 | async-start | bytes 7667712 | tf_op jit(solution)/shard_map/psum | solution.py:290
  1229.5 129.7 %copy-start.47 = (bf16[768]{0:T(1024)(128)(2,1)S(1)}, bf16[768]{0:T(1024)(128)(2,1)}, u32[]{:S(2)}) copy-start(bf16[768]{0:T(1024)(128)(2,1)} %get-tuple-element.60) | copy-start | bytes 4612
  1229.5 129.7 %copy-start.48 = (bf16[768]{0:T(1024)(128)(2,1)S(1)}, bf16[768]{0:T(1024)(128)(2,1)}, u32[]{:S(2)}) copy-start(bf16[768]{0:T(1024)(128)(2,1)} %get-tuple-element.95) | copy-start | bytes 4612
  1229.5 129.7 %copy-start.49 = (bf16[768]{0:T(1024)(128)(2,1)S(1)}, bf16[768]{0:T(1024)(128)(2,1)}, u32[]{:S(2)}) copy-start(bf16[768]{0:T(1024)(128)(2,1)} %get-tuple-element.99) | copy-start | bytes 4612
  1229.5 129.7 %copy-start.50 = (bf16[3072]{0:T(1024)(128)(2,1)S(1)}, bf16[3072]{0:T(1024)(128)(2,1)}, u32[]{:S(2)}) copy-start(bf16[3072]{0:T(1024)(128)(2,1)} %get-tuple-element.97) | copy-start | bytes 18436
  1229.5 129.7 %copy-start.54 = (bf16[768]{0:T(1024)(128)(2,1)S(1)}, bf16[768]{0:T(1024)(128)(2,1)}, u32[]{:S(2)}) copy-start(bf16[768]{0:T(1024)(128)(2,1)} %get-tuple-element.62) | copy-start | bytes 4612
  1229.5 129.7 %copy-start.55 = (bf16[768]{0:T(1024)(128)(2,1)S(1)}, bf16[768]{0:T(1024)(128)(2,1)}, u32[]{:S(2)}) copy-start(bf16[768]{0:T(1024)(128)(2,1)} %get-tuple-element.64) | copy-start | bytes 4612
  1229.5 243.6 %copy-start.3 = (f32[256,768]{1,0:T(8,128)S(1)}, f32[256,768]{1,0:T(8,128)}, u32[]{:S(2)}) copy-start(f32[256,768]{1,0:T(8,128)} %copy-done.2) | copy-start | bytes 2359300
  1229.5 243.6 %copy-start.35 = (f32[768]{0:T(1024)S(1)}, f32[768]{0:T(1024)}, u32[]{:S(2)}) copy-start(f32[768]{0:T(1024)} %convert_element_type.258) | copy-start | bytes 9220
  1229.6 243.6 %copy-start.37 = (f32[256]{0:T(256)S(1)}, f32[256]{0:T(256)}, u32[]{:S(2)}) copy-start(f32[256]{0:T(256)} %copy-done.36) | copy-start | bytes 3076
  1229.6 243.6 %copy-start.42 = (f32[256]{0:T(256)S(1)}, f32[256]{0:T(256)}, u32[]{:S(2)}) copy-start(f32[256]{0:T(256)} %copy-done.41) | copy-start | bytes 3076
  1357.0 117.2 %copy-start.17 = (f32[256,768]{1,0:T(8,128)S(1)}, f32[256,768]{1,0:T(8,128)}, u32[]{:S(2)}) copy-start(f32[256,768]{1,0:T(8,128)} %copy-done.16) | copy-start | bytes 2359300
  1357.0 117.2 %copy-start.53 = (f32[256]{0:T(256)S(1)}, f32[256]{0:T(256)}, u32[]{:S(2)}) copy-start(f32[256]{0:T(256)} %copy-done.52) | copy-start | bytes 3076
  1726.3 3.5 copy-start.24
  1726.3 5.2 copy-start.23
  (22 other events, 44.6 us)
Sparse Core Ops, SparseCore 0:
  10.4 43.0 all-gather.7
  58.0 170.9 all-gather.11
  232.3 167.3 all-gather.9
  401.8 19.3 all-gather.13
  423.2 51.2 all-gather.15
  476.6 51.7 all-gather.17
  675.2 251.2 reduce-scatter.18
  932.6 246.2 reduce-scatter.20
  1190.4 36.7 reduce-scatter.22
  1229.5 21.5 reduce-scatter.12
  1253.4 50.6 reduce-scatter.14
  1306.4 50.5 reduce-scatter.16
  1360.4 365.8 all-reduce.22
where the time goes:
time: 1750 us; the launch traced here: 1740 us
  waiting for transfers between devices  1170 us (67%)
  local copies, waits for them, and re-layouts  202 us (12%)
  matrix products  173 us (10%)
  blocking collectives  125 us (7%)
  other arithmetic  51.1 us (3%)
    unnamed x16, waiting for transfers between devices  397 us
    psum x1, waiting for transfers between devices, per_device(): lax.psum(attend_part.astype(jnp.bfloat16), 'ctx').astype(jnp.float32)  248 us
    unnamed x184, local copies, waits for them, and re-layouts  195 us
    all_gather x1, waiting for transfers between devices, per_device(): remote_keys = lax.all_gather(key_rows, 'ctx', axis=1, tiled=True)  154 us
    all_gather x1, waiting for transfers between devices, per_device(): remote_values = lax.all_gather(value_rows, 'ctx', axis=1, tiled=True)  126 us
    psum x1, blocking collectives, per_device(): lax.psum(query_bias_part.astype(jnp.bfloat16), 'ctx').astype(jnp.float32)  97.8 us
    dot_general x2, matrix products, score_block(): jnp.einsum('bqhd,bkhd->bhqk', left_rows, right_rows, preferred_element_ty...  53.5 us
    reduce_scatter x1, waiting for transfers between devices, per_device(): lax.psum_scatter(expand_term.astype(jnp.bfloat16), 'wt', scatter_dimensio...  53.1 us
  transfers between devices with their start and end apart: 13, of which 12 were waited for; matrix products, arithmetic and copies ran while one was open for 15% of the time, Pallas kernels for 0%

commit v1 on v0

v1 whole, which is shorter than its diff:
```python
import functools

import jax
import jax.numpy as jnp
from jax import lax
from jax.experimental import pallas as pl
from jax.experimental.pallas import tpu as pltpu
from jax.sharding import PartitionSpec as P

HEADS = 12
HEAD_DIM = 64
LEN = 4096
WIDTH = 768
OWNERS = 32
PAIRS = 24
SPAN = 128
MASKED = -1e30
norm_eps = 1e-06
f32 = jnp.float32
bf16 = jnp.bfloat16
MESH = pl.DeviceIdType.MESH


def layer_norm(values, gain_row, shift_row):
    centered = values - jnp.mean(values, axis=-1, keepdims=True)
    variance = jnp.mean(centered * centered, axis=-1, keepdims=True)
    return centered * lax.rsqrt(variance + norm_eps) * gain_row + shift_row


def norm_pullback(values, gain_row, upstream):
    _, pulled = jax.vjp(lambda inside, scaled: layer_norm(inside, scaled, 0.0), values, gain_row)
    grad_values, grad_gain = pulled(upstream)
    return (grad_values, grad_gain, jnp.sum(upstream, axis=0))


def exact_gelu(values):
    return jax.nn.gelu(values, approximate=False)


def dot(left, right):
    return jnp.dot(left, right, preferred_element_type=f32)


def contract(left, right, left_dim, right_dim):
    return lax.dot_general(
        left, right, (((left_dim,), (right_dim,)), ((), ())), preferred_element_type=f32
    )


def attend_kernel(len_ref, x_ref, o_ref, low_ref, lse_ref, qn, kt, vn, *, q_rows, k_rows):
    valid = len_ref[0]
    lane = lax.broadcasted_iota(jnp.int32, (64, 128), 1)
    first = lax.broadcasted_iota(jnp.int32, (64, 128), 0) == 0
    zero = jnp.zeros((64, 128), f32)
    one_row = jnp.where(first, 1.0, zero)

    @pl.when(valid > 0)
    def _():
        def prepare(c, _):
            here = pl.ds(pl.multiple_of(c * SPAN, SPAN), SPAN)
            qn[here, :] = jnp.concatenate([x_ref[c, 0].astype(f32), one_row], 0).T.astype(bf16)
            vn[here, :] = jnp.concatenate([x_ref[c, 2].astype(f32), one_row], 0).T.astype(bf16)
            kt[0:64, here] = x_ref[c, 1]
            mask = jnp.where(lane + c * SPAN < valid, 0.0, MASKED)
            kt[64:128, here] = jnp.where(first, mask, zero).astype(bf16)
            return 0

        lax.fori_loop(0, OWNERS, prepare, 0)
        k_steps = lax.div(valid + (k_rows - 1), k_rows)

        def q_block(i, _):
            q = qn[pl.ds(pl.multiple_of(i * q_rows, q_rows), q_rows), :]

            def k_block(j, carry):
                peak, acc = carry
                here = pl.ds(pl.multiple_of(j * k_rows, k_rows), k_rows)
                scores = dot(q, kt[:, here])
                folded = scores[:, 0:128]
                for t in range(1, k_rows // 128):
                    folded = jnp.maximum(folded, scores[:, t * 128 : (t + 1) * 128])
                peak_new = jnp.maximum(peak, jnp.max(folded, axis=1, keepdims=True))
                weights = jnp.exp(scores - peak_new).astype(bf16)
                return peak_new, acc * jnp.exp(peak - peak_new) + dot(weights, vn[here, :])

            start = (jnp.full((q_rows, 1), -3e38, f32), jnp.zeros((q_rows, 128), f32))
            peak, acc = lax.fori_loop(0, k_steps, k_block, start)
            total = acc[:, 64:65]
            column = lax.broadcasted_iota(jnp.int32, (q_rows, 128), 1)
            full = jnp.where(column == 64, peak + jnp.log(total), acc / total).T
            for t in range(q_rows // SPAN):
                c = i * (q_rows // SPAN) + t
                cols = slice(t * SPAN, (t + 1) * SPAN)
                o_ref[c] = full[0:64, cols]
                low_ref[c] = full[0:64, cols].astype(bf16)
                lse_ref[c] = full[64:72, cols]
            return 0

        lax.fori_loop(0, LEN // q_rows, q_block, 0)


def attend(valid, packed):
    vmem = pl.BlockSpec(memory_space=pltpu.VMEM)
    return pl.pallas_call(
        functools.partial(attend_kernel, q_rows=512, k_rows=1024),
        out_shape=(
            jax.ShapeDtypeStruct((OWNERS, 64, SPAN), f32),
            jax.ShapeDtypeStruct((OWNERS, 64, SPAN), bf16),
            jax.ShapeDtypeStruct((OWNERS, 8, SPAN), f32),
        ),
        in_specs=[pl.BlockSpec(memory_space=pltpu.SMEM), vmem],
        out_specs=[vmem] * 3,
        scratch_shapes=[
            pltpu.VMEM((LEN, 128), bf16),
            pltpu.VMEM((128, LEN), bf16),
            pltpu.VMEM((LEN, 128), bf16),
        ],
        compiler_params=pltpu.CompilerParams(vmem_limit_bytes=50 << 20),
        name="attend",
    )(valid, packed)


def split_terms(values):
    high = values.astype(bf16).astype(f32)
    rest = values - high
    middle = rest.astype(bf16).astype(f32)
    return high, middle, rest - middle


def attend_back_kernel(
    len_ref, x_ref, o_ref, lse_ref, d_ref, g_ref, qt, qn, kn, kt, vn, dt, dn, dq, *, q_rows, k_rows, streams
):
    valid = len_ref[0]

    @pl.when(valid > 0)
    def _():
        lane = lax.broadcasted_iota(jnp.int32, (64, 128), 1)
        row = lax.broadcasted_iota(jnp.int32, (64, 128), 0)
        zero = jnp.zeros((64, 128), f32)

        def prepare(c, _):
            here = pl.ds(pl.multiple_of(c * SPAN, SPAN), SPAN)
            q = x_ref[c, 0].astype(f32)
            k = x_ref[c, 1].astype(f32)
            v = x_ref[c, 2].astype(f32)
            do = d_ref[c].astype(f32)
            high, middle, rest = split_terms(-lse_ref[c][0:1])
            q_extra = jnp.where(
                row == 0, 1.0, jnp.where(row == 1, high, jnp.where(row == 2, middle, jnp.where(row == 3, rest, 0.0)))
            )
            mask = jnp.where(lane + c * SPAN < valid, 0.0, MASKED)
            k_extra = jnp.where(row == 0, mask, jnp.where(row < 4, 1.0, 0.0))
            qt[:, here] = jnp.concatenate([q, q_extra], 0).astype(bf16)
            qn[here, :] = jnp.concatenate([q, zero], 0).T.astype(bf16)
            kn[here, :] = jnp.concatenate([k, k_extra], 0).T.astype(bf16)
            kt[:, here] = k.astype(bf16)
            delta = jnp.sum(do * o_ref[c], axis=0, keepdims=True)
            high, middle, rest = split_terms(-delta)
            d_extra = jnp.where(row == 0, high, jnp.where(row == 1, middle, jnp.where(row == 2, rest, 0.0)))
            v_extra = jnp.where(row < 3, 1.0, zero)
            dt[:, here] = jnp.concatenate([do, d_extra], 0).astype(bf16)
            dn[here, :] = jnp.concatenate([do, zero], 0).T.astype(bf16)
            vn[here, :] = jnp.concatenate([v, v_extra], 0).T.astype(bf16)
            return 0

        lax.fori_loop(0, OWNERS, prepare, 0)
        dq[...] = jnp.zeros_like(dq)
        k_steps = lax.div(valid + (k_rows - 1), k_rows)
        pieces = k_rows // SPAN

        def k_block(j, _):
            here = pl.ds(pl.multiple_of(j * k_rows, k_rows), k_rows)
            k, v, k_flat = kn[here, :], vn[here, :], kt[:, here]

            def q_block(i, carry):
                dk, dv = carry
                for s in range(streams):
                    cols = pl.ds(pl.multiple_of(i * (q_rows * streams) + s * q_rows, q_rows), q_rows)
                    weights = jnp.exp(dot(k, qt[:, cols]))
                    ds = (weights * dot(v, dt[:, cols])).astype(bf16)
                    dv = dv + dot(weights.astype(bf16), dn[cols, :])
                    dk = dk + dot(ds, qn[cols, :])
                    dq[:, cols] += dot(k_flat, ds)
                return dk, dv

            start = jnp.zeros((k_rows, 128), f32)
            dk, dv = lax.fori_loop(0, LEN // (q_rows * streams), q_block, (start, start))
            for t in range(pieces):
                rows = slice(t * SPAN, (t + 1) * SPAN)
                g_ref[j * pieces + t, 1] = dk[rows].T[0:64].astype(bf16)
                g_ref[j * pieces + t, 2] = dv[rows].T[0:64].astype(bf16)
            return 0

        lax.fori_loop(0, k_steps, k_block, 0)

        def blank(j, _):
            for t in range(pieces):
                g_ref[j * pieces + t, 1] = jnp.zeros((64, 128), bf16)
                g_ref[j * pieces + t, 2] = jnp.zeros((64, 128), bf16)
            return 0

        lax.fori_loop(k_steps, LEN // k_rows, blank, 0)

        def finish(c, _):
            rounded = dq[:, pl.ds(pl.multiple_of(c * SPAN, SPAN), SPAN)].astype(bf16)
            g_ref[c, 0] = (rounded.astype(f32) * HEAD_DIM ** (-0.5)).astype(bf16)
            return 0

        lax.fori_loop(0, OWNERS, finish, 0)


def attend_back(valid, packed, mixed, lse, grad_mixed):
    vmem = pl.BlockSpec(memory_space=pltpu.VMEM)
    return pl.pallas_call(
        functools.partial(attend_back_kernel, q_rows=512, k_rows=512, streams=2),
        out_shape=jax.ShapeDtypeStruct((OWNERS, 3, 64, SPAN), bf16),
        in_specs=[pl.BlockSpec(memory_space=pltpu.SMEM)] + [vmem] * 4,
        out_specs=vmem,
        scratch_shapes=[
            pltpu.VMEM((128, LEN), bf16),
            pltpu.VMEM((LEN, 128), bf16),
            pltpu.VMEM((LEN, 128), bf16),
            pltpu.VMEM((64, LEN), bf16),
            pltpu.VMEM((LEN, 128), bf16),
            pltpu.VMEM((128, LEN), bf16),
            pltpu.VMEM((LEN, 128), bf16),
            pltpu.VMEM((64, LEN), f32),
        ],
        compiler_params=pltpu.CompilerParams(vmem_limit_bytes=50 << 20),
        name="attend_back",
    )(valid, packed, mixed, lse, grad_mixed)


def greet_owners(me):
    barrier = pltpu.get_barrier_semaphore()

    def greet(s, _):
        pl.semaphore_signal(barrier, 1, device_id={"ctx": lax.rem(me + s, OWNERS)}, device_id_type=MESH)
        return 0

    lax.fori_loop(1, OWNERS, greet, 0)
    pl.semaphore_wait(barrier, OWNERS - 1)


def token_slice(ref, pair):
    lanes = pl.ds(pl.multiple_of((pair // HEADS) * SPAN, SPAN), SPAN)
    if len(ref.shape) == 4:
        return ref.at[:, pair % HEADS, :, lanes]
    return ref.at[pair % HEADS, :, lanes]


def to_heads_kernel(src, dst, send_sem, recv_sem, local_sem):
    me = lax.axis_index("ctx")
    greet_owners(me)

    def copy(s):
        peer = lax.rem(me + s, OWNERS)
        pair = jnp.minimum(peer, PAIRS - 1)
        return peer, pltpu.make_async_remote_copy(
            token_slice(src, pair), dst.at[me], send_sem.at[s], recv_sem.at[s],
            device_id={"ctx": peer}, device_id_type=MESH,
        )

    def start(s, _):
        peer, moved = copy(s)

        @pl.when(peer < PAIRS)
        def _():
            moved.start()

        return 0

    lax.fori_loop(1, OWNERS, start, 0)

    @pl.when(me < PAIRS)
    def _():
        own = pltpu.make_async_copy(token_slice(src, jnp.minimum(me, PAIRS - 1)), dst.at[me], local_sem)
        own.start()
        own.wait()

    def finish(s, _):
        peer, moved = copy(s)

        @pl.when(peer < PAIRS)
        def _():
            moved.wait_send()

        @pl.when(me < PAIRS)
        def _():
            moved.wait_recv()

        return 0

    lax.fori_loop(1, OWNERS, finish, 0)


def to_tokens_kernel(src, dst, send_sem, recv_sem, local_sem):
    me = lax.axis_index("ctx")
    greet_owners(me)
    pair = jnp.minimum(me, PAIRS - 1)

    def copy(s):
        peer = lax.rem(me + s, OWNERS)
        return pltpu.make_async_remote_copy(
            src.at[peer], token_slice(dst, pair), send_sem.at[s], recv_sem.at[s],
            device_id={"ctx": peer}, device_id_type=MESH,
        )

    @pl.when(me < PAIRS)
    def _():
        def start(s, _):
            copy(s).start()
            return 0

        lax.fori_loop(1, OWNERS, start, 0)
        own = pltpu.make_async_copy(src.at[me], token_slice(dst, pair), local_sem)
        own.start()
        own.wait()

    def finish(s, _):
        @pl.when(me < PAIRS)
        def _():
            copy(s).wait_send()

        @pl.when(lax.rem(me + OWNERS - s, OWNERS) < PAIRS)
        def _():
            copy(s).wait_recv()

        return 0

    lax.fori_loop(1, OWNERS, finish, 0)


def exchange(kernel, values, out_shape, collective_id, name):
    anywhere = pl.BlockSpec(memory_space=pl.ANY)
    return pl.pallas_call(
        kernel,
        out_shape=jax.ShapeDtypeStruct(out_shape, bf16),
        in_specs=[anywhere],
        out_specs=anywhere,
        scratch_shapes=[
            pltpu.SemaphoreType.DMA((OWNERS,)),
            pltpu.SemaphoreType.DMA((OWNERS,)),
            pltpu.SemaphoreType.DMA(()),
        ],
        compiler_params=pltpu.CompilerParams(collective_id=collective_id, has_side_effects=True),
        name=name,
    )(values)


def place():
    ctx, wt = lax.axis_index("ctx"), lax.axis_index("wt")
    return dict(
        x_hi=ctx // 16, z=(ctx // 4) % 4, y=ctx % 4, x_lo=wt // 2, core=wt % 2, x=(ctx // 16) * 2 + wt // 2
    )


def device_at(here, **change):
    at = dict(here)
    if "x" in change:
        at["x_hi"], at["x_lo"] = change["x"] // 2, change["x"] % 2
        change = {k: v for k, v in change.items() if k != "x"}
    at.update(change)
    return (at["x_hi"] * 16 + at["z"] * 4 + at["y"], at["x_lo"] * 2 + at["core"])


def greet_all(devices):
    barrier = pltpu.get_barrier_semaphore()
    for device in devices:
        pl.semaphore_signal(barrier, 1, device_id=device, device_id_type=MESH)
    pl.semaphore_wait(barrier, len(devices))


def weights_kernel(count, *refs):
    shards, fulls = refs[:count], refs[count : 2 * count]
    send_sem, recv_sem, local_sem = refs[2 * count :]
    here = place()
    partner = device_at(here, core=1 - here["core"])
    ahead = device_at(here, x=(here["x"] + 1) % 4)
    behind = device_at(here, x=(here["x"] + 3) % 4)
    greet_all([partner, ahead, behind])
    mine = here["x_lo"] * 2 + here["core"]
    far = (1 - here["x_lo"]) * 2 + here["core"]

    def remote(src, dst, slot, n, device):
        return pltpu.make_async_remote_copy(
            src, dst, send_sem.at[slot, n], recv_sem.at[slot, n], device_id=device, device_id_type=MESH
        )

    sent, forwarded, local = [], [], []
    for n in range(count):
        rows = shards[n].shape[0]
        half = rows // 2

        def part(ref, owner, h, half=half, rows=rows):
            return ref.at[pl.ds(pl.multiple_of(owner * rows + h * half, 16), half), :]

        first = remote(shards[n].at[pl.ds(0, half), :], part(fulls[n], mine, 0), 0, n, ahead)
        second = remote(shards[n].at[pl.ds(half, half), :], part(fulls[n], mine, 1), 1, n, behind)
        whole = fulls[n].at[pl.ds(pl.multiple_of(mine * rows, 16), rows), :]
        across = remote(shards[n], whole, 2, n, partner)
        for copy in (first, second, across):
            copy.start()
        own = pltpu.make_async_copy(shards[n], whole, local_sem.at[n])
        own.start()
        local.append(own)
        sent.append((first, second, across))
        forwarded.append([remote(part(fulls[n], far, h), part(fulls[n], far, h), 3 + h, n, partner) for h in (0, 1)])
    for n in range(count):
        for h in (0, 1):
            sent[n][h].wait_recv()
            forwarded[n][h].start()
    for n in range(count):
        local[n].wait()
        for copy in sent[n]:
            copy.wait_send()
        sent[n][2].wait_recv()
        for copy in forwarded[n]:
            copy.wait()


def gather_weights(shards, collective_id):
    anywhere = pl.BlockSpec(memory_space=pl.ANY)
    count = len(shards)
    return pl.pallas_call(
        functools.partial(weights_kernel, count),
        out_shape=tuple(jax.ShapeDtypeStruct((4 * s.shape[0], s.shape[1]), s.dtype) for s in shards),
        in_specs=[anywhere] * count,
        out_specs=[anywhere] * count,
        scratch_shapes=[
            pltpu.SemaphoreType.DMA((5, count)),
            pltpu.SemaphoreType.DMA((5, count)),
            pltpu.SemaphoreType.DMA((count,)),
        ],
        compiler_params=pltpu.CompilerParams(collective_id=collective_id, has_side_effects=True),
        name="gather_weights",
    )(*shards)


ORDERS = (("y", "z", "x"), ("z", "x", "y"), ("x", "y", "z"))


def reduce_kernel(
    rows, src, out, own, other, s1, s2, s3, r1, r2, r3,
    core_send, core_recv, own_sem, send_sem, recv_sem, gather_send, gather_recv,
):
    here = place()
    partner = device_at(here, core=1 - here["core"])
    peers = {
        axis: [device_at(here, **{axis: (here[axis] + d) % 4}) for d in (1, 2, 3)] for axis in ("x", "y", "z")
    }
    opposite = 1 - here["x_hi"]
    greet_all([partner] + peers["x"] + peers["y"] + peers["z"])
    core = here["core"]

    def band(p):
        return pl.ds(p * rows, rows)

    core_copies, own_copies = [], []
    for p in range(3):
        for lo in range(2):
            moved = pltpu.make_async_remote_copy(
                src.at[lo, 1 - core, :, :, :, band(p), :], other.at[p, lo], core_send.at[p, lo], core_recv.at[p, lo],
                device_id=partner, device_id_type=MESH,
            )
            kept = pltpu.make_async_copy(src.at[lo, core, :, :, :, band(p), :], own.at[p, lo], own_sem.at[p, lo])
            moved.start()
            kept.start()
            core_copies.append(moved)
            own_copies.append(kept)

    def slot(p, stage, d):
        return (p * 3 + stage) * 3 + d

    def chunk_index(axis_list, axis, value):
        index = []
        for name in axis_list:
            if name == "x":
                index += [value % 2, value // 2] if axis == "x" else [slice(None), slice(None)]
            else:
                index.append(value if axis == name else slice(None))
        return tuple(index)

    def scatter(p, stage, source, axes, landing):
        axis = ORDERS[p][stage]
        copies = []
        for d in (1, 2, 3):
            target = (here[axis] + d) % 4
            moved = pltpu.make_async_remote_copy(
                source.at[chunk_index(axes, axis, target)], landing.at[d - 1],
                send_sem.at[slot(p, stage, d - 1)], recv_sem.at[slot(p, stage, d - 1)],
                device_id=peers[axis][d - 1], device_id_type=MESH,
            )
            moved.start()
            copies.append(moved)
        return copies

    def sums(p, stage, source, axes, landing, target):
        axis = ORDERS[p][stage]
        kept = source.at[chunk_index(axes, axis, here[axis])]
        lead = target.shape[:-2]
        total = 1
        for size in lead:
            total *= size

        def step(n, _):
            index, left = [], n
            for size in reversed(lead):
                index.insert(0, left % size)
                left = left // size
            index = tuple(index)
            value = kept[index].astype(f32)
            for d in range(3):
                value = value + landing[(d,) + index].astype(f32)
            target[index] = value.astype(bf16)
            return 0

        if lead:
            lax.fori_loop(0, total, step, 0)
        else:
            value = kept[...].astype(f32)
            for d in range(3):
                value = value + landing[d].astype(f32)
            target[...] = value.astype(bf16)

    left_axes = []
    for p in range(3):
        axes = ["x", "z", "y"]
        left = [list(axes)]
        for axis in ORDERS[p]:
            axes.remove(axis)
            left.append(list(axes))
        left_axes.append(left)

    in_flight = [None] * 3
    for p in range(3):
        for lo in range(2):
            own_copies[2 * p + lo].wait()
            core_copies[2 * p + lo].wait_recv()

        def add(n, _, p=p):
            lo, hi, z, y = n // 32, (n // 16) % 2, (n // 4) % 4, n % 4
            index = (p, lo, hi, z, y)
            own[index] = (own[index].astype(f32) + other[index].astype(f32)).astype(bf16)
            return 0

        lax.fori_loop(0, 64, add, 0)
        in_flight[p] = scatter(p, 0, own.at[p], left_axes[p][0], r1[p])
    waits = []
    stages = ((own, r1, s1), (None, r2, s2), (None, r3, s3))
    for stage in range(3):
        for p in range(3):
            source = own.at[p] if stage == 0 else (s1[p] if stage == 1 else s2[p])
            landing = (r1, r2, r3)[stage][p]
            target = (s1, s2, s3)[stage][p]
            for moved in in_flight[p]:
                moved.wait_recv()
            waits += in_flight[p]
            if stage < 2:
                sums(p, stage, source, left_axes[p][stage], landing, target)
                in_flight[p] = scatter(p, stage + 1, target, left_axes[p][stage + 1], (r1, r2, r3)[stage + 1][p])
            else:
                final = out.at[here["x_hi"], here["z"], here["y"], band(p), :]
                sums(p, stage, source, left_axes[p][stage], landing, final)

    def spread(p, stage):
        axis = ORDERS[p][2 - stage]
        done = [ORDERS[p][2 - k] for k in range(stage)]
        index = tuple(
            slice(None) if name in done else here["x_hi" if name == "x" else name] for name in ("x", "z", "y")
        )
        piece = out.at[index + (band(p), slice(None))]
        if axis == "x":
            targets = [device_at(here, x_hi=opposite)]
        else:
            targets = peers[axis]
        copies = []
        for d, device in enumerate(targets):
            moved = pltpu.make_async_remote_copy(
                piece, piece, gather_send.at[slot(p, stage, d)], gather_recv.at[slot(p, stage, d)],
                device_id=device, device_id_type=MESH,
            )
            moved.start()
            copies.append(moved)
        return copies

    for stage in range(3):
        for p in range(3):
            if stage:
                for moved in in_flight[p]:
                    moved.wait_recv()
                waits += in_flight[p]
            in_flight[p] = spread(p, stage)
    for p in range(3):
        for moved in in_flight[p]:
            moved.wait_recv()
        waits += in_flight[p]
    for moved in waits + core_copies:
        moved.wait_send()


def reduce_gradients(values, rows, collective_id):
    def stage_shapes(lead):
        out = []
        for p in range(3):
            axes = ["x", "z", "y"]
            for axis in ORDERS[p][:lead]:
                axes.remove(axis)
            shape = []
            for name in axes:
                shape += [2, 2] if name == "x" else [4]
            out.append(tuple(shape) + (rows, 128))
        return out

    after = [stage_shapes(n) for n in (1, 2, 3)]
    scratch = [pltpu.VMEM((3, 2, 2, 4, 4, rows, 128), bf16), pltpu.VMEM((3, 2, 2, 4, 4, rows, 128), bf16)]
    for shapes in after[:2]:
        scratch += [pltpu.VMEM(shape, bf16) for shape in shapes]
    for shapes in after:
        scratch += [pltpu.VMEM((3,) + shape, bf16) for shape in shapes]
    scratch += [
        pltpu.SemaphoreType.DMA((3, 2)), pltpu.SemaphoreType.DMA((3, 2)), pltpu.SemaphoreType.DMA((3, 2)),
        pltpu.SemaphoreType.DMA((27,)), pltpu.SemaphoreType.DMA((27,)),
        pltpu.SemaphoreType.DMA((27,)), pltpu.SemaphoreType.DMA((27,)),
    ]

    def kernel(src, out, own, other, a0, a1, a2, b0, b1, b2, c0, c1, c2, d0, d1, d2, e0, e1, e2, *sems):
        reduce_kernel(
            rows, src, out, own, other, (a0, a1, a2), (b0, b1, b2), (None,) * 3,
            (c0, c1, c2), (d0, d1, d2), (e0, e1, e2), *sems,
        )

    return pl.pallas_call(
        kernel,
        out_shape=jax.ShapeDtypeStruct((2, 4, 4, 3 * rows, 128), bf16),
        in_specs=[pl.BlockSpec(memory_space=pl.ANY)],
        out_specs=pl.BlockSpec(memory_space=pltpu.VMEM),
        scratch_shapes=scratch,
        compiler_params=pltpu.CompilerParams(
            collective_id=collective_id, has_side_effects=True, vmem_limit_bytes=50 << 20
        ),
        name="reduce_gradients",
    )(values)


def columns_out(matrix):
    rows, width = matrix.shape
    blocks = matrix.astype(bf16).reshape(4, rows // 4, width // 128, 128)
    return jnp.transpose(blocks, (0, 2, 1, 3)).reshape(4, -1, 128)


def columns_in(flat, rows, width):
    blocks = flat.astype(f32).reshape(width // 128, rows, 128)
    return jnp.transpose(blocks, (1, 0, 2)).reshape(rows, width)


def per_device(
    inputs, lengths, attend_weight, query_bias, value_bias, output_weight, output_bias, norm_gain, norm_shift,
    expand_weight, expand_bias, shrink_weight, shrink_bias, final_gain, final_shift, cotangent,
):
    ctx, wt = lax.axis_index("ctx"), lax.axis_index("wt")
    vectors = (
        query_bias, value_bias, output_bias, norm_gain, norm_shift, expand_bias, shrink_bias, final_gain, final_shift,
    )
    small = jnp.concatenate([v.astype(bf16) for v in vectors] + [jnp.zeros((32 * 128 - 2304,), bf16)]).reshape(32, 128)
    attend_full, small_full, output_full, expand_full, shrink_full = gather_weights(
        (attend_weight.astype(bf16), small, output_weight.astype(bf16), expand_weight.astype(bf16),
         shrink_weight.astype(bf16)), 0,
    )
    small_full = small_full.reshape(4, 32 * 128).astype(f32)
    unpacked, offset = [], 0
    for v in vectors:
        unpacked.append(small_full[:, offset : offset + v.shape[0]].reshape(-1))
        offset += v.shape[0]
    query_add, value_add, output_add, gain_one, shift_one, expand_add, shrink_add, gain_two, shift_two = unpacked

    seq_count, tok_local, model_width = inputs.shape
    row_count = seq_count * tok_local
    tokens = inputs.reshape(row_count, model_width)
    tokens_low = tokens.astype(bf16)
    column_scale = jnp.concatenate(
        [jnp.full((model_width,), HEAD_DIM ** (-0.5), f32), jnp.ones((2 * model_width,), f32)]
    )
    bias = jnp.concatenate([query_add, jnp.zeros_like(query_add), value_add])
    packed = ((contract(attend_full, tokens_low, 0, 1) + bias[:, None]) * column_scale[:, None]).astype(bf16)
    held = exchange(to_heads_kernel, packed.reshape(3, HEADS, 64, row_count), (OWNERS, 3, 64, SPAN), 1, "to_heads")
    my_length = jnp.where(ctx < HEADS, lengths[0], lengths[1])
    my_length = jnp.where(ctx < PAIRS, my_length, 0).astype(jnp.int32).reshape(1)
    mixed_heads, mixed_heads_low, lse = attend(my_length, held)
    mixed_low = exchange(
        to_tokens_kernel, mixed_heads_low, (HEADS, 64, row_count), 2, "mixed_to_tokens"
    ).reshape(model_width, row_count)

    attended = contract(mixed_low, output_full, 0, 0) + output_add
    hidden_one = tokens + attended
    normed_one = layer_norm(hidden_one, gain_one, shift_one)
    normed_low = normed_one.astype(bf16)
    raised = dot(normed_low, expand_full) + expand_add
    activated = exact_gelu(raised).astype(bf16)
    branch = dot(activated, shrink_full) + shrink_add
    hidden_two = normed_one + branch
    result = layer_norm(hidden_two, gain_two, shift_two)

    upstream = cotangent.reshape(row_count, model_width)
    grad_two, final_gain_term, final_shift_term = norm_pullback(hidden_two, gain_two, upstream)
    branch_low = grad_two.astype(bf16)
    shrink_bias_term = jnp.sum(branch_low.astype(f32), axis=0)
    shrink_term = contract(activated, branch_low, 0, 0)
    grad_active = contract(branch_low, shrink_full, 1, 1)
    _, gelu_pull = jax.vjp(exact_gelu, raised)
    raised_low = gelu_pull(grad_active)[0].astype(bf16)
    expand_bias_term = jnp.sum(raised_low.astype(f32), axis=0)
    expand_term = contract(normed_low, raised_low, 0, 0)
    grad_normed = grad_two + contract(raised_low, expand_full, 1, 1)
    grad_one, norm_gain_term, norm_shift_term = norm_pullback(hidden_one, gain_one, grad_normed)
    attended_low = grad_one.astype(bf16)
    output_bias_term = jnp.sum(attended_low.astype(f32), axis=0)
    output_term = dot(mixed_low, attended_low)
    grad_mixed = contract(output_full, attended_low, 1, 1).astype(bf16)

    grad_heads = exchange(
        to_heads_kernel, grad_mixed.reshape(HEADS, 64, row_count), (OWNERS, 64, SPAN), 3, "grad_to_heads"
    )
    grad_held = attend_back(my_length, held, mixed_heads, lse, grad_heads)
    grad_packed = exchange(
        to_tokens_kernel, grad_held, (3, HEADS, 64, row_count), 4, "grad_to_tokens"
    ).reshape(3 * model_width, row_count)
    attend_term = contract(tokens_low, grad_packed, 0, 1)
    input_grad = grad_one + contract(grad_packed, attend_full, 0, 1)
    query_bias_term = jnp.sum(grad_packed[:model_width].astype(f32), axis=1)
    value_bias_term = jnp.sum(grad_packed[2 * model_width :].astype(f32), axis=1)

    packed_terms = jnp.concatenate(
        [columns_out(m) for m in (output_term, expand_term, shrink_term, attend_term)], axis=1
    )
    total = packed_terms.shape[1]
    reduced = reduce_gradients(
        packed_terms.reshape(2, 2, 2, 4, 4, total // 32, 128), total // 96, 5
    ).reshape(total, 128)
    grads, offset = [], 0
    for rows, width in ((192, 768), (192, 3072), (768, 768), (192, 2304)):
        count = rows * width // 128
        grads.append(columns_in(reduced[offset : offset + count], rows, width))
        offset += count
    output_grad, expand_grad, shrink_grad, attend_grad = grads

    early = lax.psum(
        jnp.concatenate(
            [t.reshape(4, -1) for t in (
                output_bias_term, norm_gain_term, norm_shift_term, expand_bias_term, shrink_bias_term,
                final_gain_term, final_shift_term)], axis=1,
        ), ("ctx", "wt"),
    )
    late = lax.psum(
        jnp.concatenate([t.reshape(4, -1) for t in (query_bias_term, value_bias_term)], axis=1), ("ctx", "wt")
    )
    early = lax.dynamic_index_in_dim(early, wt, 0, keepdims=False)
    late = lax.dynamic_index_in_dim(late, wt, 0, keepdims=False)
    n = 192
    return (
        result.reshape(inputs.shape),
        input_grad.reshape(inputs.shape),
        attend_grad,
        late[:n],
        late[n:],
        output_grad,
        early[0:n],
        early[n : 2 * n],
        early[2 * n : 3 * n],
        expand_grad,
        early[3 * n : 7 * n],
        shrink_grad,
        early[7 * n : 8 * n],
        early[8 * n : 9 * n],
        early[9 * n : 10 * n],
    )


def solution(mesh):
    wide, rows, flat = P("wt", "ctx", None), P("wt", None), P("wt")
    return jax.shard_map(
        per_device,
        mesh=mesh,
        in_specs=(
            wide, flat, rows, flat, flat, rows, flat, flat, flat, rows, flat, rows, flat, flat, flat, wide,
        ),
        out_specs=(
            wide, wide, rows, flat, flat, rows, flat, flat, flat, rows, flat, rows, flat, flat, flat,
        ),
        check_vma=False,
    )
```

time: 1750 us -> 607 us (0.35)
  waiting for transfers between devices: 1170 us -> 0 us
  Pallas kernels: 0 us -> 368 us
  local copies, waits for them, and re-layouts: 202 us -> 73.1 us
  matrix products: 173 us -> 44.3 us
  blocking collectives: 125 us -> 69.6 us
    all_gather x6 -> x0, waiting for transfers between devices: 399 us -> none  [the longest x1 154 us: per_device(): remote_keys = lax.all_gather(key_rows, 'ctx', axis=1, tiled=True)]
    unnamed x16 -> x0, waiting for transfers between devices: 397 us -> none
    pallas_call x0 -> x8, Pallas kernels: none -> 368 us  [the longest x1 112 us: gather_weights(): pl.pallas_call(functools.partial(weights_kernel, count), out_shape=tuple(...]
    psum x1 -> x0, waiting for transfers between devices: 248 us -> none  [per_device(): lax.psum(attend_part.astype(jnp.bfloat16), 'ctx').astype(jnp.float32)]
    unnamed x184 -> x72, local copies, waits for them, and re-layouts: 195 us -> 10.1 us
    dot_general x18 -> x12, matrix products: 173 us -> 44.3 us  [the longest x9 29.9 us: contract(): lax.dot_general(left, right, (((left_dim,), (right_dim,)), ((), ())), pre...]
    reduce_scatter x3 -> x0, waiting for transfers between devices: 127 us -> none  [the longest x1 53.1 us: per_device(): lax.psum_scatter(expand_term.astype(jnp.bfloat16), 'wt', scatter_dimensio...]
    psum x1, blocking collectives: 97.8 us -> 69.6 us  [per_device(): lax.psum(jnp.concatenate([t.reshape(4, -1) for t in (query_bias_term, val...]
  transfers between devices with their start and end apart: 13 -> 0, of which waited for: 12 -> 0; matrix products, arithmetic and copies ran while one was open for 15% -> 0% of each run, Pallas kernels for 0% -> 0%
where the time goes in v1:
time: 607 us; the launch traced here: 600 us
  Pallas kernels  368 us (61%)
  local copies, waits for them, and re-layouts  73.1 us (12%)
  blocking collectives  69.6 us (11%)
  matrix products  44.3 us (7%)
  other arithmetic  42.9 us (7%)
    pallas_call x1, Pallas kernels, gather_weights(): pl.pallas_call(functools.partial(weights_kernel, count), out_shape=tuple(...  112 us
    pallas_call x4, Pallas kernels, exchange(): pl.pallas_call(kernel, out_shape=jax.ShapeDtypeStruct(out_shape, bf16), i...  86.7 us
    pallas_call x1, Pallas kernels, reduce_gradients(): pl.pallas_call(kernel, out_shape=jax.ShapeDtypeStruct((2, 4, 4, 3 * rows,...  83.3 us
    psum x1, blocking collectives, per_device(): lax.psum(jnp.concatenate([t.reshape(4, -1) for t in (query_bias_term, val...  69.6 us
    pallas_call x1, Pallas kernels, attend_back(): pl.pallas_call(functools.partial(attend_back_kernel, q_rows=512, k_rows=5...  51.6 us
    pallas_call x1, Pallas kernels, attend(): pl.pallas_call(functools.partial(attend_kernel, q_rows=512, k_rows=1024),...  34 us
    dot_general x9, matrix products, contract(): lax.dot_general(left, right, (((left_dim,), (right_dim,)), ((), ())), pre...  29.9 us
    reshape x3, local copies, waits for them, and re-layouts, columns_out(): blocks = matrix.astype(bf16).reshape(4, rows // 4, width // 128, 128)  19.7 us

profile of v1, /device:TPU:0, one launch (start us, length us, event | category | flops | bytes accessed | tf_op | source)
XLA Modules:
  0.0 600.4 jit_solution(16740960830719567035)
XLA Ops:
  0.7 0.8 convert_element_type.111
  1.5 0.7 convert_element_type.112
  2.2 0.7 convert_element_type.113
  2.9 0.7 convert_element_type.114
  4.9 0.7 convert_element_type.118
  6.3 1.3 fusion.26
  8.9 0.7 convert_element_type.116
  9.6 1.2 reduce_sum.176
  11.5 0.7 concatenate.15
  12.1 1.8 convert_element_type.120.refs_2_
  13.9 2.2 fusion.22
  16.2 2.6 convert_element_type.110.refs_0_
  18.8 1.2 convert_element_type.121.refs_3_
  20.0 1.1 convert_element_type.122.refs_4_
  21.1 111.9 %gather_weights.1 = (bf16[768,2304]{1,0:T(8,128)(2,1)}, bf16[128,128]{1,0:T(8,128)(2,1)}, bf16[768,768]{1,0:T(8,128)(2,1)}, bf16[768,3072]{1,0:T(8,128)(2,1)}, bf16[3072,768]{1,0:T(8,128)(2,1)}) custom-call(bf16[192,2304]{1,0:T(8,128)(2,1)} %convert_element_type.110.refs_0_, bf16[32,128]{1,0:T(8,128)(2,1)} %bitcast.129, ...), custom_call_target="tpu_custom_call" | custom-call | tf_op jit(solution)/shard_map/gather_weights/pallas_call | solution.py:424
  133.0 0.8 reshape.289
  135.8 4.6 fusion.2
  140.4 31.9 %to_heads.1.x_ref = bf16[32,3,64,128]{3,2,1,0:T(8,128)(2,1)} custom-call(bf16[3,12,64,256]{3,2,1,0:T(8,128)(2,1)} %bitcast.126), custom_call_target="tpu_custom_call" | custom-call | tf_op jit(solution)/shard_map/to_heads/pallas_call | solution.py:335
  172.3 1.4 copy-done
  173.7 34.0 %attend.1 = (f32[32,64,128]{2,1,0:T(8,128)S(1)}, bf16[32,64,128]{2,1,0:T(8,128)(2,1)S(1)}, f32[32,8,128]{2,1,0:T(8,128)S(1)}) custom-call(s32[1]{0:T(128)} %bitcast.3.len_ref, bf16[32,3,64,128]{3,2,1,0:T(8,128)(2,1)S(1)} %copy-done), custom_call_target="tpu_custom_call" | custom-call | tf_op jit(solution)/shard_map/attend/pallas_call | solution.py:103
  207.7 0.8 copy-done.3
  208.5 10.7 %mixed_to_tokens.1 = bf16[12,64,256]{2,1,0:T(8,128)(2,1)} custom-call(bf16[32,64,128]{2,1,0:T(8,128)(2,1)} %copy-done.3), custom_call_target="tpu_custom_call" | custom-call | tf_op jit(solution)/shard_map/mixed_to_tokens/pallas_call | solution.py:335
  219.2 2.1 fusion.27
  221.6 11.4 %multiply_convert_fusion = (bf16[256,3072]{1,0:T(8,128)(2,1)S(1)}, f32[256,3072]{1,0:T(8,128)}, f32[256,3072]{1,0:T(8,128)}) fusion(f32[3072]{0:T(1024)S(1)} %add.112, bf16[768,3072]{1,0:T(8,128)(2,1)} %get-tuple-element.27, f32[256,768]{1,0:T(8,128)S(1)} %get-tuple-element.106, f32[768]{0:T(1024)S(1)} %add.109, f32[768]{0:T(1024)S(1)} %mul.165, ...), kind=kOutput, calls=%fused_computation.14 | convolution fusion | flops 1260847104 | bytes 13389824 | tf_op jit(solution)/shard_map/dot_general | solution.py:41
  233.1 1.5 fusion.28
  235.5 0.9 fusion.12
  236.3 1.4 reshape.281
  237.7 0.9 multiply_multiply_fusion.6
  238.5 2.1 fusion.19
  240.8 5.6 convert_reduce_fusion
  246.5 2.5 multiply_reduce_fusion
  249.2 1.5 fusion.18
  250.9 2.5 convolution_convert_fusion.4
  253.6 0.7 concatenate.19
  254.3 17.8 %grad_to_heads.1.d_ref = bf16[32,64,128]{2,1,0:T(8,128)(2,1)} custom-call(bf16[12,64,256]{2,1,0:T(8,128)(2,1)} %bitcast.128), custom_call_target="tpu_custom_call" | custom-call | tf_op jit(solution)/shard_map/grad_to_heads/pallas_call | solution.py:335
  272.0 1.0 copy-done.2
  273.1 51.6 %attend_back.1.src = bf16[32,3,64,128]{3,2,1,0:T(8,128)(2,1)S(1)} custom-call(s32[1]{0:T(128)} %bitcast.3.len_ref, bf16[32,3,64,128]{3,2,1,0:T(8,128)(2,1)} %to_heads.1.x_ref, f32[32,64,128]{2,1,0:T(8,128)S(1)} %get-tuple-element.29.o_ref, f32[32,8,128]{2,1,0:T(8,128)S(1)} %get-tuple-element.30.lse_ref, bf16[32,64,128]{2,1,0:T(8,128)(2,1)S(1)} %copy-done.2), custom_call_target="tpu_custom_call" | custom-call | tf_op jit(solution)/shard_map/attend_back/pallas_call | solution.py:213
  324.7 1.1 copy-done.1
  325.9 26.4 %grad_to_tokens.1 = bf16[3,12,64,256]{3,2,1,0:T(8,128)(2,1)} custom-call(bf16[32,3,64,128]{3,2,1,0:T(8,128)(2,1)} %copy-done.1), custom_call_target="tpu_custom_call" | custom-call | tf_op jit(solution)/shard_map/grad_to_tokens/pallas_call | solution.py:335
  352.3 4.5 convolution_add_fusion.3
  357.3 69.6 %all-reduce = (f32[4,384]{1,0:T(4,128)S(1)}, f32[4,1920]{1,0:T(4,128)S(1)}) all-reduce(f32[4,384]{1,0:T(4,128)S(1)} %pad_maximum_fusion.2, f32[4,1920]{1,0:T(4,128)} %concatenate.19), channel_id=1, replica_groups=mesh['ctx'=32,'wt'=4] {'ctx','wt'}, use_global_device_ids=true, to_apply=%region_10.11 | all-reduce | flops 9216 | bytes 73728 | tf_op jit(solution)/shard_map/psum | solution.py:753
  427.6 0.7 dynamic-slice_reduce_fusion
  428.3 1.5 convolution_convert_fusion.3
  429.8 2.8 reshape.258
  432.6 1.3 copy.44
  434.4 1.6 fusion.9
  436.0 1.4 copy.58
  437.4 0.8 bitcast_bitcast_fusion
  438.2 3.3 copy.45
  441.6 2.8 fusion
  444.4 5.8 copy.48
  450.2 7.1 %reshape.264 = bf16[4,192,18,128]{3,2,1,0:T(8,128)(2,1)} reshape(bf16[768,2304]{1,0:T(8,128)(2,1)} %copy.48) | data formatting | bytes 7077888 | tf_op jit(solution)/shard_map/reshape | solution.py:647
  457.3 5.2 copy.49
  462.6 3.6 convolution_convert_fusion.1
  466.2 6.6 %copy.46 = bf16[3072,768]{0,1:T(8,128)(2,1)} copy(bf16[3072,768]{1,0:T(8,128)(2,1)} %convolution_convert_fusion.1) | data formatting | bytes 9437184 | tf_op jit(solution)/shard_map/convert_element_type | solution.py:647
  472.8 9.8 %reshape.262 = bf16[4,768,6,128]{1,0,3,2:T(4,128)(2,1)} reshape(bf16[3072,768]{0,1:T(8,128)(2,1)} %copy.46) | data formatting | bytes 9437184 | tf_op jit(solution)/shard_map/reshape | solution.py:647
  482.6 8.8 %copy.47 = bf16[4,6,768,128]{3,2,1,0:T(8,128)(2,1)} copy(bf16[4,6,768,128]{2,0,3,1:T(4,128)(2,1)} %bitcast.110) | data formatting | bytes 9437184 | tf_op jit(solution)/shard_map/transpose | solution.py:648
  491.3 16.0 %pad_maximum_fusion = bf16[4,13824,128]{2,1,0:T(8,128)(2,1)} fusion(bf16[4,3456,128]{2,1,0:T(8,128)(2,1)} %bitcast.112, bf16[4,4608,128]{2,1,0:T(8,128)(2,1)} %bitcast.108, bf16[4,4608,128]{2,1,0:T(8,128)(2,1)} %bitcast.107, bf16[4,1152,128]{2,1,0:T(8,128)(2,1)S(1)} %bitcast.117), kind=kLoop, calls=%fused_computation | loop fusion | flops 56623104 | bytes 28311552 | tf_op jit(solution)/shard_map/concatenate | solution.py:732
  507.4 83.3 %reduce_gradients.1 = bf16[2,4,4,432,128]{4,3,2,1,0:T(8,128)(2,1)S(1)} custom-call(bf16[2,2,2,4,4,432,128]{6,5,4,3,2,1,0:T(8,128)(2,1)} %bitcast.106), custom_call_target="tpu_custom_call" | custom-call | tf_op jit(solution)/shard_map/reduce_gradients/pallas_call | solution.py:632
  590.7 0.9 copy_bitcast_fusion.2
  591.8 1.3 copy_bitcast_fusion.1
  593.1 1.7 copy_bitcast_fusion
  594.9 2.0 copy.53
  596.9 3.0 copy.54
  (111 shorter events, 8.6 us)
Async XLA Ops:
  0.6 18.1 %copy-start.11 = (f32[192,3072]{1,0:T(8,128)S(1)}, f32[192,3072]{1,0:T(8,128)}, u32[]{:S(2)}) copy-start(f32[192,3072]{1,0:T(8,128)} %param.25) | copy-start | bytes 7077892
  16.2 3.8 copy-start.12
  20.0 115.8 %copy-start.29 = (f32[2304]{0:T(1024)S(1)}, f32[2304]{0:T(1024)}, u32[]{:S(2)}) copy-start(f32[2304]{0:T(1024)} %constant.18.clone.1) | copy-start | bytes 27652
  140.4 78.8 %copy-start.10 = (f32[2,128,768]{2,1,0:T(8,128)S(1)}, f32[2,128,768]{2,1,0:T(8,128)}, u32[]{:S(2)}) copy-start(f32[2,128,768]{2,1,0:T(8,128)} %param.16) | copy-start | bytes 2359300
  172.3 1.4 copy-start
  207.7 0.8 copy-start.3
  219.2 13.8 %slice-start.2 = ((s8[4718592]{0:T(1024)(128)(4,1)}), s8[4194304]{0:T(1024)(128)(4,1)S(1)}, s32[]{:S(2)}) async-start(s8[4718592]{0:T(1024)(128)(4,1)} %bitcast.140), calls=%async_computation.2 | async-start | bytes 8388608
  221.6 11.5 %copy-start.23 = (f32[256]{0:T(256)}, f32[256]{0:T(256)S(1)}, u32[]{:S(2)}) copy-start(f32[256]{0:T(256)S(1)} %multiply_reduce_fusion.4) | copy-start | bytes 3076
  221.6 11.4 %copy-start.18 = (f32[256]{0:T(256)}, f32[256]{0:T(256)S(1)}, u32[]{:S(2)}) copy-start(f32[256]{0:T(256)S(1)} %fusion.14) | copy-start | bytes 3076
  221.6 11.4 %copy-start.27 = (f32[768]{0:T(1024)S(1)}, f32[768]{0:T(1024)}, u32[]{:S(2)}) copy-start(f32[768]{0:T(1024)} %add.115) | copy-start | bytes 9220
  221.6 11.4 %slice-start.3 = ((s8[4718592]{0:T(1024)(128)(4,1)}), s8[524288]{0:T(1024)(128)(4,1)S(1)}, s32[]{:S(2)}) async-start(s8[4718592]{0:T(1024)(128)(4,1)} %bitcast.140), calls=%async_computation.3 | async-start | bytes 1048576
  233.0 1.6 copy-start.7
  233.1 2.4 copy-start.5
  234.6 0.8 copy-start.22
  234.9 0.6 copy-start.25
  235.5 0.9 copy-start.26
  237.7 3.1 copy-start.30
  238.5 8.0 %slice-start = ((s8[4718592]{0:T(1024)(128)(4,1)}), s8[4194304]{0:T(1024)(128)(4,1)S(1)}, s32[]{:S(2)}) async-start(s8[4718592]{0:T(1024)(128)(4,1)} %bitcast.138), calls=%async_computation | async-start | bytes 8388608
  240.8 5.7 copy-start.14
  240.8 5.7 copy-start.19
  240.8 5.7 slice-start.1
  246.5 2.6 copy-start.16
  246.5 2.6 copy-start.24
  249.1 4.5 copy-start.20
  249.1 4.5 copy-start.21
  250.7 2.8 copy-start.28
  272.0 1.0 copy-start.2
  324.7 1.1 copy-start.1
  352.3 4.5 copy-start.4
  352.3 76.0 %copy-start.9 = (bf16[12,64,256]{2,1,0:T(8,128)(2,1)S(1)}, bf16[12,64,256]{2,1,0:T(8,128)(2,1)}, u32[]{:S(2)}) copy-start(bf16[12,64,256]{2,1,0:T(8,128)(2,1)} %mixed_to_tokens.1) | copy-start | bytes 1179652
  432.6 1.8 copy-start.17
  438.2 3.3 copy-start.13
  457.3 5.2 copy-start.8
  457.3 5.2 copy-start.15
  482.6 8.8 %copy-start.6 = (bf16[4,6,192,128]{3,2,1,0:T(8,128)(2,1)S(1)}, bf16[4,6,192,128]{3,2,1,0:T(8,128)(2,1)}, u32[]{:S(2)}) copy-start(bf16[4,6,192,128]{3,2,1,0:T(8,128)(2,1)} %copy.44) | copy-start | bytes 3538948

commit v2 on v1

v2 whole, which is shorter than its diff:
```python
import functools

import jax
import jax.numpy as jnp
from jax import lax
from jax.experimental import pallas as pl
from jax.experimental.pallas import tpu as pltpu
from jax.sharding import PartitionSpec as P

HEADS = 12
HEAD_DIM = 64
LEN = 4096
WIDTH = 768
OWNERS = 32
PAIRS = 24
VMEM_BYTES = 58 << 20
SPAN = 128
MASKED = -1e30
norm_eps = 1e-06
f32 = jnp.float32
bf16 = jnp.bfloat16
MESH = pl.DeviceIdType.MESH


def layer_norm(values, gain_row, shift_row):
    centered = values - jnp.mean(values, axis=-1, keepdims=True)
    variance = jnp.mean(centered * centered, axis=-1, keepdims=True)
    return centered * lax.rsqrt(variance + norm_eps) * gain_row + shift_row


def norm_pullback(values, gain_row, upstream):
    _, pulled = jax.vjp(lambda inside, scaled: layer_norm(inside, scaled, 0.0), values, gain_row)
    grad_values, grad_gain = pulled(upstream)
    return (grad_values, grad_gain, jnp.sum(upstream, axis=0))


def exact_gelu(values):
    return jax.nn.gelu(values, approximate=False)


def dot(left, right):
    return jnp.dot(left, right, preferred_element_type=f32)


def contract(left, right, left_dim, right_dim):
    return lax.dot_general(
        left, right, (((left_dim,), (right_dim,)), ((), ())), preferred_element_type=f32
    )


def head_of(ctx):
    z, y = (ctx // 4) % 4, ctx % 4
    turn = lax.rem(y + 7 - z, 4)
    return ctx // 16, 3 * z + jnp.minimum(turn, 2), turn < 3


def greet_owners(me):
    barrier = pltpu.get_barrier_semaphore()

    def greet(s, _):
        pl.semaphore_signal(barrier, 1, device_id={"ctx": lax.rem(me + s, OWNERS)}, device_id_type=MESH)
        return 0

    lax.fori_loop(1, OWNERS, greet, 0)
    pl.semaphore_wait(barrier, OWNERS - 1)


def token_slice(ref, ctx):
    seq, head, _ = head_of(ctx)
    lanes = pl.ds(pl.multiple_of(seq * SPAN, SPAN), SPAN)
    if len(ref.shape) == 4:
        return ref.at[:, head, :, lanes]
    return ref.at[head, :, lanes]


def to_heads_kernel(src, dst, send_sem, recv_sem, local_sem):
    me = lax.axis_index("ctx")
    greet_owners(me)
    holds = head_of(me)[2]

    def copy(s):
        peer = lax.rem(me + s, OWNERS)
        return head_of(peer)[2], pltpu.make_async_remote_copy(
            token_slice(src, peer), dst.at[me], send_sem.at[s], recv_sem.at[s],
            device_id={"ctx": peer}, device_id_type=MESH,
        )

    def start(s, _):
        wanted, moved = copy(s)

        @pl.when(wanted)
        def _():
            moved.start()

        return 0

    lax.fori_loop(1, OWNERS, start, 0)

    @pl.when(holds)
    def _():
        own = pltpu.make_async_copy(token_slice(src, me), dst.at[me], local_sem)
        own.start()
        own.wait()

    def finish(s, _):
        wanted, moved = copy(s)

        @pl.when(wanted)
        def _():
            moved.wait_send()

        @pl.when(holds)
        def _():
            moved.wait_recv()

        return 0

    lax.fori_loop(1, OWNERS, finish, 0)


def to_tokens_kernel(src, dst, send_sem, recv_sem, local_sem):
    me = lax.axis_index("ctx")
    greet_owners(me)
    holds = head_of(me)[2]

    def copy(s):
        peer = lax.rem(me + s, OWNERS)
        return pltpu.make_async_remote_copy(
            src.at[peer], token_slice(dst, me), send_sem.at[s], recv_sem.at[s],
            device_id={"ctx": peer}, device_id_type=MESH,
        )

    @pl.when(holds)
    def _():
        def start(s, _):
            copy(s).start()
            return 0

        lax.fori_loop(1, OWNERS, start, 0)
        own = pltpu.make_async_copy(src.at[me], token_slice(dst, me), local_sem)
        own.start()
        own.wait()

    def finish(s, _):
        @pl.when(holds)
        def _():
            copy(s).wait_send()

        @pl.when(head_of(lax.rem(me + OWNERS - s, OWNERS))[2])
        def _():
            copy(s).wait_recv()

        return 0

    lax.fori_loop(1, OWNERS, finish, 0)


def exchange(kernel, values, out_shape, collective_id, name):
    anywhere = pl.BlockSpec(memory_space=pl.ANY)
    return pl.pallas_call(
        kernel,
        out_shape=jax.ShapeDtypeStruct(out_shape, bf16),
        in_specs=[anywhere],
        out_specs=anywhere,
        scratch_shapes=[
            pltpu.SemaphoreType.DMA((OWNERS,)),
            pltpu.SemaphoreType.DMA((OWNERS,)),
            pltpu.SemaphoreType.DMA(()),
        ],
        compiler_params=pltpu.CompilerParams(collective_id=collective_id, has_side_effects=True),
        name=name,
    )(values)


def place():
    ctx, wt = lax.axis_index("ctx"), lax.axis_index("wt")
    return dict(
        x_hi=ctx // 16, z=(ctx // 4) % 4, y=ctx % 4, x_lo=wt // 2, core=wt % 2, x=(ctx // 16) * 2 + wt // 2
    )


def device_at(here, **change):
    at = dict(here)
    if "x" in change:
        at["x_hi"], at["x_lo"] = change["x"] // 2, change["x"] % 2
        change = {k: v for k, v in change.items() if k != "x"}
    at.update(change)
    return (at["x_hi"] * 16 + at["z"] * 4 + at["y"], at["x_lo"] * 2 + at["core"])


def greet_all(devices):
    barrier = pltpu.get_barrier_semaphore()
    for device in devices:
        pl.semaphore_signal(barrier, 1, device_id=device, device_id_type=MESH)
    pl.semaphore_wait(barrier, len(devices))


class WeightGather:
    def __init__(self, here, shards, fulls, send_sem, recv_sem, local_sem):
        self.partner = device_at(here, core=1 - here["core"])
        self.ahead = device_at(here, x=(here["x"] + 1) % 4)
        self.behind = device_at(here, x=(here["x"] + 3) % 4)
        self.mine = here["x_lo"] * 2 + here["core"]
        self.far = (1 - here["x_lo"]) * 2 + here["core"]
        self.shards, self.fulls = shards, fulls
        self.sems = send_sem, recv_sem, local_sem

    def neighbours(self):
        return [self.partner, self.ahead, self.behind]

    def remote(self, src, dst, slot, n, device):
        return pltpu.make_async_remote_copy(
            src, dst, self.sems[0].at[slot, n], self.sems[1].at[slot, n], device_id=device, device_id_type=MESH
        )

    def start(self):
        self.sent, self.local, self.handed = [], [], []
        for n, (shard, full) in enumerate(zip(self.shards, self.fulls)):
            rows = shard.shape[0]
            half = rows // 2

            def part(owner, h, full=full, rows=rows, half=half):
                return full.at[pl.ds(pl.multiple_of(owner * rows + h * half, 16), half), :]

            whole = full.at[pl.ds(pl.multiple_of(self.mine * rows, 16), rows), :]
            copies = [
                self.remote(shard.at[pl.ds(0, half), :], part(self.mine, 0), 0, n, self.ahead),
                self.remote(shard.at[pl.ds(half, half), :], part(self.mine, 1), 1, n, self.behind),
                self.remote(shard, whole, 2, n, self.partner),
            ]
            own = pltpu.make_async_copy(shard, whole, self.sems[2].at[n])
            for copy in copies + [own]:
                copy.start()
            self.sent.append(copies)
            self.local.append(own)
            self.handed.append(
                [self.remote(part(self.far, h), part(self.far, h), 3 + h, n, self.partner) for h in (0, 1)]
            )

    def hand_on(self, n):
        for h in (0, 1):
            self.sent[n][h].wait_recv()
            self.handed[n][h].start()

    def finish(self):
        for copies, own, handed in zip(self.sent, self.local, self.handed):
            own.wait()
            for copy in copies:
                copy.wait_send()
            copies[2].wait_recv()
            for copy in handed:
                copy.wait()


def first_weights_kernel(weight, *refs):
    vectors, (full, small_full, low, small, small_low, send_sem, recv_sem, local_sem) = refs[:9], refs[9:]
    here = place()
    gather = WeightGather(here, (low, small_low), (full, small_full), send_sem, recv_sem, local_sem)
    low[...] = weight[...].astype(bf16)
    small[...] = jnp.zeros_like(small)
    for n, vector in enumerate(vectors):
        small[n : n + 1, 0 : vector.shape[1]] = vector[...]
    small_low[...] = small[...].astype(bf16)
    greet_all(gather.neighbours())
    gather.start()
    gather.hand_on(0)
    gather.hand_on(1)
    gather.finish()


def first_weights(weight, vectors, collective_id):
    vmem, anywhere = pl.BlockSpec(memory_space=pltpu.VMEM), pl.BlockSpec(memory_space=pl.ANY)
    rows, width = weight.shape
    return pl.pallas_call(
        first_weights_kernel,
        out_shape=(jax.ShapeDtypeStruct((4 * rows, width), bf16), jax.ShapeDtypeStruct((128, 768), bf16)),
        in_specs=[vmem] * 10,
        out_specs=[anywhere] * 2,
        scratch_shapes=[
            pltpu.VMEM((rows, width), bf16), pltpu.VMEM((32, 768), f32), pltpu.VMEM((32, 768), bf16),
            pltpu.SemaphoreType.DMA((5, 2)), pltpu.SemaphoreType.DMA((5, 2)), pltpu.SemaphoreType.DMA((2,)),
        ],
        compiler_params=pltpu.CompilerParams(
            collective_id=collective_id, has_side_effects=True, vmem_limit_bytes=VMEM_BYTES
        ),
        name="first_weights",
    )(weight, *[v.reshape(1, -1) for v in vectors])


def attend_kernel(
    len_ref, x_ref, w0, w1, w2, o_ref, low_ref, lse_ref, f0, f1, f2, qn, kt, vn, b0, b1, b2,
    send_sem, recv_sem, local_sem, *, q_rows, k_rows,
):
    valid = len_ref[0]
    gather = WeightGather(place(), (b0, b1, b2), (f0, f1, f2), send_sem, recv_sem, local_sem)
    for low, wide in ((b0, w0), (b1, w1), (b2, w2)):
        low[...] = wide[...].astype(bf16)
    greet_all(gather.neighbours())
    gather.start()
    lane = lax.broadcasted_iota(jnp.int32, (64, 128), 1)
    first = lax.broadcasted_iota(jnp.int32, (64, 128), 0) == 0
    zero = jnp.zeros((64, 128), f32)
    one_row = jnp.where(first, 1.0, zero)

    def prepare(c, _):
        here = pl.ds(pl.multiple_of(c * SPAN, SPAN), SPAN)
        qn[here, :] = jnp.concatenate([x_ref[c, 0].astype(f32), one_row], 0).T.astype(bf16)
        vn[here, :] = jnp.concatenate([x_ref[c, 2].astype(f32), one_row], 0).T.astype(bf16)
        kt[0:64, here] = x_ref[c, 1]
        mask = jnp.where(lane + c * SPAN < valid, 0.0, MASKED)
        kt[64:128, here] = jnp.where(first, mask, zero).astype(bf16)
        return 0

    lax.fori_loop(0, OWNERS, prepare, 0)

    def q_block(i, _):
        q = qn[pl.ds(pl.multiple_of(i * q_rows, q_rows), q_rows), :]

        def k_block(j, carry):
            peak, acc = carry
            here = pl.ds(pl.multiple_of(j * k_rows, k_rows), k_rows)
            scores = dot(q, kt[:, here])
            folded = scores[:, 0:128]
            for t in range(1, k_rows // 128):
                folded = jnp.maximum(folded, scores[:, t * 128 : (t + 1) * 128])
            peak_new = jnp.maximum(peak, jnp.max(folded, axis=1, keepdims=True))
            weights = jnp.exp(scores - peak_new).astype(bf16)
            return peak_new, acc * jnp.exp(peak - peak_new) + dot(weights, vn[here, :])

        start = (jnp.full((q_rows, 1), -3e38, f32), jnp.zeros((q_rows, 128), f32))
        peak, acc = lax.fori_loop(0, LEN // k_rows, k_block, start)
        total = acc[:, 64:65]
        column = lax.broadcasted_iota(jnp.int32, (q_rows, 128), 1)
        full = jnp.where(column == 64, peak + jnp.log(total), acc / total).T
        for t in range(q_rows // SPAN):
            c = i * (q_rows // SPAN) + t
            cols = slice(t * SPAN, (t + 1) * SPAN)
            o_ref[c] = full[0:64, cols]
            low_ref[c] = full[0:64, cols].astype(bf16)
            lse_ref[c] = full[64:72, cols]
        return 0

    steps = LEN // q_rows
    cuts = (0, steps // 2, steps - 2, steps)
    for n in range(3):
        lax.fori_loop(cuts[n], cuts[n + 1], q_block, 0)
        gather.hand_on(n)
    gather.finish()


def attend(valid, packed, shards, collective_id):
    vmem, anywhere = pl.BlockSpec(memory_space=pltpu.VMEM), pl.BlockSpec(memory_space=pl.ANY)
    return pl.pallas_call(
        functools.partial(attend_kernel, q_rows=512, k_rows=1024),
        out_shape=(
            jax.ShapeDtypeStruct((OWNERS, 64, SPAN), f32),
            jax.ShapeDtypeStruct((OWNERS, 64, SPAN), bf16),
            jax.ShapeDtypeStruct((OWNERS, 8, SPAN), f32),
        ) + tuple(jax.ShapeDtypeStruct((4 * s.shape[0], s.shape[1]), bf16) for s in shards),
        in_specs=[pl.BlockSpec(memory_space=pltpu.SMEM)] + [vmem] * 4,
        out_specs=[vmem] * 3 + [anywhere] * 3,
        scratch_shapes=[
            pltpu.VMEM((LEN, 128), bf16),
            pltpu.VMEM((128, LEN), bf16),
            pltpu.VMEM((LEN, 128), bf16),
        ] + [pltpu.VMEM(s.shape, bf16) for s in shards] + [
            pltpu.SemaphoreType.DMA((5, 3)), pltpu.SemaphoreType.DMA((5, 3)), pltpu.SemaphoreType.DMA((3,)),
        ],
        compiler_params=pltpu.CompilerParams(
            collective_id=collective_id, has_side_effects=True, vmem_limit_bytes=VMEM_BYTES
        ),
        name="attend",
    )(valid, packed, *shards)


def split_terms(values):
    high = values.astype(bf16).astype(f32)
    rest = values - high
    middle = rest.astype(bf16).astype(f32)
    return high, middle, rest - middle


def attend_back_body(
    len_ref, x_ref, o_ref, lse_ref, d_ref, g_ref, qt, qn, kn, kt, vn, dt, dn, dq, *, q_rows, k_rows, streams, after
):
    valid = len_ref[0]
    lane = lax.broadcasted_iota(jnp.int32, (64, 128), 1)
    row = lax.broadcasted_iota(jnp.int32, (64, 128), 0)
    zero = jnp.zeros((64, 128), f32)

    def prepare(c, _):
        here = pl.ds(pl.multiple_of(c * SPAN, SPAN), SPAN)
        q = x_ref[c, 0].astype(f32)
        k = x_ref[c, 1].astype(f32)
        v = x_ref[c, 2].astype(f32)
        do = d_ref[c].astype(f32)
        high, middle, rest = split_terms(-lse_ref[c][0:1])
        q_extra = jnp.where(
            row == 0, 1.0, jnp.where(row == 1, high, jnp.where(row == 2, middle, jnp.where(row == 3, rest, 0.0)))
        )
        mask = jnp.where(lane + c * SPAN < valid, 0.0, MASKED)
        k_extra = jnp.where(row == 0, mask, jnp.where(row < 4, 1.0, 0.0))
        qt[:, here] = jnp.concatenate([q, q_extra], 0).astype(bf16)
        qn[here, :] = jnp.concatenate([q, zero], 0).T.astype(bf16)
        kn[here, :] = jnp.concatenate([k, k_extra], 0).T.astype(bf16)
        kt[:, here] = k.astype(bf16)
        delta = jnp.sum(do * o_ref[c], axis=0, keepdims=True)
        high, middle, rest = split_terms(-delta)
        d_extra = jnp.where(row == 0, high, jnp.where(row == 1, middle, jnp.where(row == 2, rest, 0.0)))
        v_extra = jnp.where(row < 3, 1.0, zero)
        dt[:, here] = jnp.concatenate([do, d_extra], 0).astype(bf16)
        dn[here, :] = jnp.concatenate([do, zero], 0).T.astype(bf16)
        vn[here, :] = jnp.concatenate([v, v_extra], 0).T.astype(bf16)
        return 0

    lax.fori_loop(0, OWNERS, prepare, 0)
    dq[...] = jnp.zeros_like(dq)
    pieces = k_rows // SPAN

    def k_block(j, _):
        here = pl.ds(pl.multiple_of(j * k_rows, k_rows), k_rows)
        k, v, k_flat = kn[here, :], vn[here, :], kt[:, here]

        def q_block(i, carry):
            dk, dv = carry
            for s in range(streams):
                cols = pl.ds(pl.multiple_of(i * (q_rows * streams) + s * q_rows, q_rows), q_rows)
                weights = jnp.exp(dot(k, qt[:, cols]))
                ds = (weights * dot(v, dt[:, cols])).astype(bf16)
                dv = dv + dot(weights.astype(bf16), dn[cols, :])
                dk = dk + dot(ds, qn[cols, :])
                dq[:, cols] += dot(k_flat, ds)
            return dk, dv

        start = jnp.zeros((k_rows, 128), f32)
        dk, dv = lax.fori_loop(0, LEN // (q_rows * streams), q_block, (start, start))
        for t in range(pieces):
            rows = slice(t * SPAN, (t + 1) * SPAN)
            g_ref[j * pieces + t, 1] = dk[rows].T[0:64].astype(bf16)
            g_ref[j * pieces + t, 2] = dv[rows].T[0:64].astype(bf16)
        return 0

    begin = 0
    for end, event in after:
        lax.fori_loop(begin, end, k_block, 0)
        event()
        begin = end

    def finish(c, _):
        rounded = dq[:, pl.ds(pl.multiple_of(c * SPAN, SPAN), SPAN)].astype(bf16)
        g_ref[c, 0] = (rounded.astype(f32) * HEAD_DIM ** (-0.5)).astype(bf16)
        return 0

    lax.fori_loop(0, OWNERS, finish, 0)


ORDERS = (("y", "z", "x"), ("z", "x", "y"), ("x", "y", "z"))
LEAD = ("x", "z", "y")
STAGES = ("y", "z", "x")


def axes_after(p, count):
    return [a for a in LEAD if a not in ORDERS[p][:count]]


def shape_after(p, count, width):
    shape = []
    for name in axes_after(p, count):
        shape += [2, 2] if name == "x" else [4]
    return tuple(shape) + (16, width)


def total_shape(width):
    return (2, 4, 4, 48, width)


class Reduce:
    def __init__(self, here, width, halves, merge, unpack, small, scratch):
        self.here, self.width, self.merge, self.unpack, self.small = here, width, merge, unpack, small
        self.halves = halves
        (self.acc, self.out, self.sums, self.landing, self.hall,
         self.core_send, self.core_recv, self.own_sem, self.send_sem, self.recv_sem,
         self.back_send, self.back_recv, self.small_send, self.small_recv) = scratch
        self.partner = device_at(here, core=1 - here["core"])
        self.peers = {
            axis: [device_at(here, **{axis: (here[axis] + d) % 4}) for d in (1, 2, 3)] for axis in STAGES
        }
        self.waits = []
        self.flying = [[], [], []]

    @staticmethod
    def scratch(width, halves, small_rows):
        shapes = []
        for shape in halves:
            shapes += [pltpu.VMEM((3, 2) + shape, bf16)] * 2
        shapes += [pltpu.VMEM(shape_after(p, 0, width), bf16) for p in range(3)]
        shapes.append(pltpu.VMEM(total_shape(width), bf16))
        for count in (1, 2):
            shapes += [pltpu.VMEM(shape_after(p, count, width), bf16) for p in range(3)]
        for count in (1, 2, 3):
            shapes += [pltpu.VMEM((3,) + shape_after(p, count, width), bf16) for p in range(3)]
        shapes.append(pltpu.VMEM((4, 4, small_rows, 128), f32))
        count = 3 * 2 * len(halves)
        shapes += [pltpu.SemaphoreType.DMA((count,))] * 3
        shapes += [pltpu.SemaphoreType.DMA((27,))] * 4
        shapes += [pltpu.SemaphoreType.DMA((12,))] * 2
        return shapes

    @staticmethod
    def unflatten(refs, tensors):
        refs = list(refs)
        pairs = [(refs[2 * n], refs[2 * n + 1]) for n in range(tensors)]
        refs = refs[2 * tensors :]
        acc, out, refs = refs[:3], refs[3], refs[4:]
        sums = [refs[0:3], refs[3:6]]
        landing = [refs[6:9], refs[9:12], refs[12:15]]
        return pairs, [acc, out, sums, landing] + refs[15:]

    def neighbours(self):
        return [self.partner] + [device for axis in STAGES for device in self.peers[axis]]

    def remote(self, src, dst, sems, slot, device):
        copy = pltpu.make_async_remote_copy(
            src, dst, sems[0].at[slot], sems[1].at[slot], device_id=device, device_id_type=MESH
        )
        copy.start()
        self.waits.append(copy)
        return copy

    def start(self):
        core = self.here["core"]
        self.core_copies = [[], [], []]
        slot = 0
        for p in range(3):
            for source, own, other in self.halves:
                for lo in range(2):
                    moved = self.remote(
                        source.at[lo, 1 - core, p], other.at[p, lo], (self.core_send, self.core_recv), slot,
                        self.partner,
                    )
                    kept = pltpu.make_async_copy(source.at[lo, core, p], own.at[p, lo], self.own_sem.at[slot])
                    kept.start()
                    self.core_copies[p].append((moved, kept))
                    slot += 1
        self.small_stage(0, self.small[...])

    def small_stage(self, stage, value):
        axis = STAGES[stage] if stage < 3 else "core"
        mine = self.hall.at[stage, self.here[axis]]
        mine[...] = value
        devices = self.peers[axis] if stage < 3 else [self.partner]
        self.small_flying = [
            self.remote(mine, mine, (self.small_send, self.small_recv), 3 * stage + d, device)
            for d, device in enumerate(devices)
        ]

    def small_sum(self, stage):
        for copy in self.small_flying:
            copy.wait_recv()
        value = self.hall[stage, 0]
        for n in range(1, 4 if stage < 3 else 2):
            value = value + self.hall[stage, n]
        return value

    def index(self, axes, axis, value):
        index = []
        for name in axes:
            if name == "x":
                index += [value % 2, value // 2] if axis == "x" else [slice(None), slice(None)]
            else:
                index.append(value if axis == name else slice(None))
        return tuple(index)

    def scatter(self, p, stage, source):
        axis, axes = ORDERS[p][stage], axes_after(p, stage)
        self.flying[p] = [
            self.remote(
                source.at[self.index(axes, axis, (self.here[axis] + d) % 4)], self.landing[stage][p].at[d - 1],
                (self.send_sem, self.recv_sem), (p * 3 + stage) * 3 + d - 1, self.peers[axis][d - 1],
            )
            for d in (1, 2, 3)
        ]

    def begin(self, p):
        for moved, kept in self.core_copies[p]:
            moved.wait_recv()
            kept.wait()
        self.merge(p, self.acc[p])
        self.scatter(p, 0, self.acc[p])

    def advance(self, p, stage):
        axis, axes = ORDERS[p][stage], axes_after(p, stage)
        source = self.acc[p] if stage == 0 else self.sums[stage - 1][p]
        kept = source.at[self.index(axes, axis, self.here[axis])]
        landing = self.landing[stage][p]
        for copy in self.flying[p]:
            copy.wait_recv()
        if stage < 2:
            target = self.sums[stage][p]
        else:
            target = self.out.at[self.here["x_hi"], self.here["z"], self.here["y"], pl.ds(16 * p, 16), :]
        lead = target.shape[:-2]
        total = 1
        for size in lead:
            total *= size

        def step(n, _):
            index, left = [], n
            for size in reversed(lead):
                index.insert(0, left % size)
                left = left // size
            index = tuple(index)
            value = kept[index].astype(f32)
            for d in range(3):
                value = value + landing[(d,) + index].astype(f32)
            target[index] = value.astype(bf16)
            return 0

        if lead:
            lax.fori_loop(0, total, step, 0)
            self.scatter(p, stage + 1, target)
        else:
            value = kept[...].astype(f32)
            for d in range(3):
                value = value + landing[d].astype(f32)
            target[...] = value.astype(bf16)
            self.spread(p, 0)

    def spread(self, p, stage):
        if stage:
            for copy in self.flying[p]:
                copy.wait_recv()
        if stage == 3:
            return
        axis = ORDERS[p][2 - stage]
        done = [ORDERS[p][2 - k] for k in range(stage)]
        index = tuple(
            slice(None) if name in done else self.here["x_hi" if name == "x" else name] for name in LEAD
        )
        piece = self.out.at[index + (pl.ds(16 * p, 16), slice(None))]
        devices = [device_at(self.here, x_hi=1 - self.here["x_hi"])] if axis == "x" else self.peers[axis]
        self.flying[p] = [
            self.remote(piece, piece, (self.back_send, self.back_recv), (p * 3 + stage) * 3 + d, device)
            for d, device in enumerate(devices)
        ]

    def step(self, number):
        for p in range(3):
            if number == 0:
                self.begin(p)
            elif number <= 3:
                self.advance(p, number - 1)
            else:
                self.spread(p, number - 3)
        if 1 <= number <= 3:
            self.small_stage(number, self.small_sum(number - 1))
        elif number == 4:
            self.small[...] = self.small_sum(3)

    def finish(self):
        self.unpack(self.out)
        for copy in self.waits:
            copy.wait_send()


def merge_blocks(p, pairs, acc, blocks):
    def step(n, _):
        lo, z = n // 4, n % 4

        def load(tensor, index):
            own, other = pairs[tensor]
            index = (p, lo, z) + index
            return own[index].astype(f32) + other[index].astype(f32)

        for (hi, y, left), value in blocks(load):
            acc[lo, hi, z, y, :, left : left + value.shape[1]] = value.astype(bf16)
        return 0

    lax.fori_loop(0, 8, step, 0)


def cut(value):
    return [value[:, n * 384 : (n + 1) * 384] for n in range(value.shape[1] // 384)]


def early_blocks(load):
    wide = cut(load(0, ()))
    found = [((n // 4, n % 4, 0), value) for n, value in enumerate(wide)]
    for y in range(4):
        found += [((hi, y, 384), value) for hi, value in enumerate(cut(load(1, (y,))))]
    return found


def late_blocks(load):
    pieces = cut(load(0, ())) + cut(load(1, ()))
    return [((n // 4, n % 4, 0), value) for n, value in enumerate(pieces)]


def early_unpack(expand_out, shrink_out):
    def unpack(out):
        def step(n, _):
            p, z = n // 4, n % 4
            band = pl.ds(pl.multiple_of(p * 16, 16), 16)
            rows = pl.ds(pl.multiple_of(n * 16, 16), 16)
            for hi in range(2):
                for y in range(4):
                    value = out[hi, z, y, band, :].astype(f32)
                    left = hi * 1536 + y * 384
                    expand_out[rows, left : left + 384] = value[:, 0:384]
                    below = pl.ds(pl.multiple_of(n * 64 + y * 16, 16), 16)
                    shrink_out[below, hi * 384 : hi * 384 + 384] = value[:, 384:768]
            return 0

        lax.fori_loop(0, 12, step, 0)

    return unpack


def late_unpack(output_out, attend_out):
    def unpack(out):
        def step(n, _):
            p, z = n // 4, n % 4
            band = pl.ds(pl.multiple_of(p * 16, 16), 16)
            rows = pl.ds(pl.multiple_of(n * 16, 16), 16)
            for m in range(8):
                value = out[m // 4, z, m % 4, band, :].astype(f32)
                if m < 2:
                    output_out[rows, m * 384 : m * 384 + 384] = value
                else:
                    attend_out[rows, (m - 2) * 384 : (m - 1) * 384] = value
            return 0

        lax.fori_loop(0, 12, step, 0)

    return unpack


EARLY_HALVES = ((4, 16, 3072), (4, 4, 16, 768))
LATE_HALVES = ((4, 16, 768), (4, 16, 2304))


def attend_back_kernel(
    len_ref, x_ref, o_ref, lse_ref, d_ref, expand_src, shrink_src, small_src,
    g_ref, expand_out, shrink_out, small_out, *refs,
):
    attention, refs = refs[:8], refs[8:]
    pairs, scratch = Reduce.unflatten(refs, 2)
    small_out[...] = small_src[...]
    reduce = Reduce(
        place(), 768, [(source, *pair) for source, pair in zip((expand_src, shrink_src), pairs)],
        lambda p, acc: merge_blocks(p, pairs, acc, early_blocks), early_unpack(expand_out, shrink_out),
        small_out, scratch,
    )
    greet_all(reduce.neighbours())
    reduce.start()
    after = ((1, 0), (5, 1), (6, 2), (7, 3), (8, 4))
    attend_back_body(
        len_ref, x_ref, o_ref, lse_ref, d_ref, g_ref, *attention, q_rows=512, k_rows=512, streams=2,
        after=[(end, functools.partial(reduce.step, number)) for end, number in after],
    )
    reduce.step(5)
    reduce.step(6)
    reduce.finish()


def attend_back(valid, packed, mixed, lse, grad_mixed, expand_term, shrink_term, small, collective_id):
    vmem, anywhere = pl.BlockSpec(memory_space=pltpu.VMEM), pl.BlockSpec(memory_space=pl.ANY)
    return pl.pallas_call(
        attend_back_kernel,
        out_shape=(
            jax.ShapeDtypeStruct((OWNERS, 3, 64, SPAN), bf16),
            jax.ShapeDtypeStruct((192, 3072), f32),
            jax.ShapeDtypeStruct((768, 768), f32),
            jax.ShapeDtypeStruct(small.shape, f32),
        ),
        in_specs=[pl.BlockSpec(memory_space=pltpu.SMEM)] + [vmem] * 4 + [anywhere] * 2 + [vmem],
        out_specs=[vmem] * 4,
        scratch_shapes=[
            pltpu.VMEM((128, LEN), bf16),
            pltpu.VMEM((LEN, 128), bf16),
            pltpu.VMEM((LEN, 128), bf16),
            pltpu.VMEM((64, LEN), bf16),
            pltpu.VMEM((LEN, 128), bf16),
            pltpu.VMEM((128, LEN), bf16),
            pltpu.VMEM((LEN, 128), bf16),
            pltpu.VMEM((64, LEN), f32),
        ] + Reduce.scratch(768, EARLY_HALVES, small.shape[0]),
        compiler_params=pltpu.CompilerParams(
            collective_id=collective_id, has_side_effects=True, vmem_limit_bytes=VMEM_BYTES
        ),
        name="attend_back",
    )(
        valid, packed, mixed, lse, grad_mixed, expand_term.reshape(2, 2, 3, 4, 16, 3072),
        shrink_term.reshape(2, 2, 3, 4, 4, 16, 768), small,
    )


def late_kernel(output_src, attend_src, small_src, output_out, attend_out, small_out, *refs):
    pairs, scratch = Reduce.unflatten(refs, 2)
    small_out[...] = small_src[...]
    reduce = Reduce(
        place(), 384, [(source, *pair) for source, pair in zip((output_src, attend_src), pairs)],
        lambda p, acc: merge_blocks(p, pairs, acc, late_blocks), late_unpack(output_out, attend_out),
        small_out, scratch,
    )
    greet_all(reduce.neighbours())
    reduce.start()
    for number in range(7):
        reduce.step(number)
    reduce.finish()


def late_reduce(output_term, attend_term, small, collective_id):
    vmem, anywhere = pl.BlockSpec(memory_space=pltpu.VMEM), pl.BlockSpec(memory_space=pl.ANY)
    return pl.pallas_call(
        late_kernel,
        out_shape=(
            jax.ShapeDtypeStruct((192, 768), f32),
            jax.ShapeDtypeStruct((192, 2304), f32),
            jax.ShapeDtypeStruct(small.shape, f32),
        ),
        in_specs=[anywhere] * 2 + [vmem],
        out_specs=[vmem] * 3,
        scratch_shapes=Reduce.scratch(384, LATE_HALVES, small.shape[0]),
        compiler_params=pltpu.CompilerParams(
            collective_id=collective_id, has_side_effects=True, vmem_limit_bytes=VMEM_BYTES
        ),
        name="late_reduce",
    )(output_term.reshape(2, 2, 3, 4, 16, 768), attend_term.reshape(2, 2, 3, 4, 16, 2304), small)


def per_device(
    inputs, lengths, attend_weight, query_bias, value_bias, output_weight, output_bias, norm_gain, norm_shift,
    expand_weight, expand_bias, shrink_weight, shrink_bias, final_gain, final_shift, cotangent,
):
    ctx, wt = lax.axis_index("ctx"), lax.axis_index("wt")
    vectors = (
        query_bias, value_bias, output_bias, norm_gain, norm_shift, expand_bias, shrink_bias, final_gain, final_shift,
    )
    attend_full, small_full = first_weights(attend_weight, vectors, 0)
    small_full = small_full.reshape(4, 32, 768).astype(f32)
    query_add, value_add, output_add, gain_one, shift_one, expand_add, shrink_add, gain_two, shift_two = [
        small_full[:, n, : v.shape[0]].reshape(-1) for n, v in enumerate(vectors)
    ]

    seq_count, tok_local, model_width = inputs.shape
    row_count = seq_count * tok_local
    tokens = inputs.reshape(row_count, model_width)
    tokens_low = tokens.astype(bf16)
    column_scale = jnp.concatenate(
        [jnp.full((model_width,), HEAD_DIM ** (-0.5), f32), jnp.ones((2 * model_width,), f32)]
    )
    bias = jnp.concatenate([query_add, jnp.zeros_like(query_add), value_add])
    packed = ((contract(attend_full, tokens_low, 0, 1) + bias[:, None]) * column_scale[:, None]).astype(bf16)
    held = exchange(to_heads_kernel, packed.reshape(3, HEADS, 64, row_count), (OWNERS, 3, 64, SPAN), 1, "to_heads")
    seq, _, holds = head_of(ctx)
    my_length = jnp.where(holds, lengths[seq], 0).astype(jnp.int32).reshape(1)
    mixed_heads, mixed_heads_low, lse, output_full, expand_full, shrink_full = attend(
        my_length, held, (output_weight, expand_weight, shrink_weight), 6
    )
    mixed_low = exchange(
        to_tokens_kernel, mixed_heads_low, (HEADS, 64, row_count), 2, "mixed_to_tokens"
    ).reshape(model_width, row_count)

    attended = contract(mixed_low, output_full, 0, 0) + output_add
    hidden_one = tokens + attended
    normed_one = layer_norm(hidden_one, gain_one, shift_one)
    normed_low = normed_one.astype(bf16)
    raised = dot(normed_low, expand_full) + expand_add
    activated = exact_gelu(raised).astype(bf16)
    branch = dot(activated, shrink_full) + shrink_add
    hidden_two = normed_one + branch
    result = layer_norm(hidden_two, gain_two, shift_two)

    upstream = cotangent.reshape(row_count, model_width)
    grad_two, final_gain_term, final_shift_term = norm_pullback(hidden_two, gain_two, upstream)
    branch_low = grad_two.astype(bf16)
    shrink_bias_term = jnp.sum(branch_low.astype(f32), axis=0)
    shrink_term = contract(activated, branch_low, 0, 0)
    grad_active = contract(branch_low, shrink_full, 1, 1)
    _, gelu_pull = jax.vjp(exact_gelu, raised)
    raised_low = gelu_pull(grad_active)[0].astype(bf16)
    expand_bias_term = jnp.sum(raised_low.astype(f32), axis=0)
    expand_term = contract(normed_low, raised_low, 0, 0)
    grad_normed = grad_two + contract(raised_low, expand_full, 1, 1)
    grad_one, norm_gain_term, norm_shift_term = norm_pullback(hidden_one, gain_one, grad_normed)
    attended_low = grad_one.astype(bf16)
    output_bias_term = jnp.sum(attended_low.astype(f32), axis=0)
    output_term = dot(mixed_low, attended_low)
    grad_mixed = contract(output_full, attended_low, 1, 1).astype(bf16)

    grad_heads = exchange(
        to_heads_kernel, grad_mixed.reshape(HEADS, 64, row_count), (OWNERS, 64, SPAN), 3, "grad_to_heads"
    )
    early = jnp.concatenate(
        [t.reshape(4, -1) for t in (
            output_bias_term, norm_gain_term, norm_shift_term, expand_bias_term, shrink_bias_term,
            final_gain_term, final_shift_term)] + [jnp.zeros((4, 128), f32)], axis=1,
    ).reshape(64, 128)
    grad_held, expand_grad, shrink_grad, early = attend_back(
        my_length, held, mixed_heads, lse, grad_heads, expand_term.astype(bf16), shrink_term.astype(bf16), early, 5
    )
    grad_packed = exchange(
        to_tokens_kernel, grad_held, (3, HEADS, 64, row_count), 4, "grad_to_tokens"
    ).reshape(3 * model_width, row_count)
    attend_term = contract(tokens_low, grad_packed, 0, 1)
    input_grad = grad_one + contract(grad_packed, attend_full, 0, 1)
    query_bias_term = jnp.sum(grad_packed[:model_width].astype(f32), axis=1)
    value_bias_term = jnp.sum(grad_packed[2 * model_width :].astype(f32), axis=1)

    late = jnp.concatenate(
        [t.reshape(4, -1) for t in (query_bias_term, value_bias_term)] + [jnp.zeros((4, 128), f32)], axis=1
    ).reshape(16, 128)
    output_grad, attend_grad, late = late_reduce(output_term.astype(bf16), attend_term.astype(bf16), late, 7)
    early = lax.dynamic_index_in_dim(early.reshape(4, 2048), wt, 0, keepdims=False)
    late = lax.dynamic_index_in_dim(late.reshape(4, 512), wt, 0, keepdims=False)
    n = 192
    return (
        result.reshape(inputs.shape),
        input_grad.reshape(inputs.shape),
        attend_grad,
        late[:n],
        late[n : 2 * n],
        output_grad,
        early[0:n],
        early[n : 2 * n],
        early[2 * n : 3 * n],
        expand_grad,
        early[3 * n : 7 * n],
        shrink_grad,
        early[7 * n : 8 * n],
        early[8 * n : 9 * n],
        early[9 * n : 10 * n],
    )


def solution(mesh):
    wide, rows, flat = P("wt", "ctx", None), P("wt", None), P("wt")
    return jax.shard_map(
        per_device,
        mesh=mesh,
        in_specs=(
            wide, flat, rows, flat, flat, rows, flat, flat, flat, rows, flat, rows, flat, flat, flat, wide,
        ),
        out_specs=(
            wide, wide, rows, flat, flat, rows, flat, flat, flat, rows, flat, rows, flat, flat, flat,
        ),
        check_vma=False,
    )
```

time: 607 us -> 342 us (0.56); the launches traced: 600 us -> 342 us
  Pallas kernels: 368 us -> 268 us
  blocking collectives: 69.6 us -> 0 us
  local copies, waits for them, and re-layouts: 73.1 us -> 14.8 us
  other arithmetic: 42.9 us -> 6.72 us
    pallas_call x3, Pallas kernels: 247 us -> 147 us  [the longest x1 81.3 us: attend_back(): pl.pallas_call(attend_back_kernel, out_shape=(jax.ShapeDtypeStruct((OWNER...]
    psum x1 -> x0, blocking collectives: 69.6 us -> none  [per_device(): lax.psum(jnp.concatenate([t.reshape(4, -1) for t in (query_bias_term, val...]
    transpose x5 -> x0, local copies, waits for them, and re-layouts: 19.4 us -> none  [columns_out(): return jnp.transpose(blocks, (0, 2, 1, 3)).reshape(4, -1, 128)]
    reshape x6 -> x5, local copies, waits for them, and re-layouts: 21.9 us -> 3.47 us  [the longest x1 1.34 us: first_weights(): v.reshape(1, -1)]
    concatenate x1 -> x0, other arithmetic: 16 us -> none  [per_device(): jnp.concatenate([columns_out(m) for m in (output_term, expand_term, shrin...]
    convert_element_type x3 -> x0, local copies, waits for them, and re-layouts: 13.2 us -> none  [the longest x2 12.4 us: columns_out(): blocks = matrix.astype(bf16).reshape(4, rows // 4, width // 128, 128)]
    convert_element_type x13 -> x1, other arithmetic: 13 us -> 0.96 us  [per_device(): small_full = small_full.reshape(4, 32, 768).astype(f32)]
    pallas_call x1, Pallas kernels: 34 us -> 43.8 us  [attend(): pl.pallas_call(functools.partial(attend_kernel, q_rows=512, k_rows=1024),...]
where the time goes in v2:
time: 342 us
  Pallas kernels  268 us (78%)
  matrix products  49.9 us (15%)
  local copies, waits for them, and re-layouts  14.8 us (4%)
  other arithmetic  6.72 us (2%)
    pallas_call x1, Pallas kernels, attend_back(): pl.pallas_call(attend_back_kernel, out_shape=(jax.ShapeDtypeStruct((OWNER...  81.3 us
    pallas_call x4, Pallas kernels, exchange(): pl.pallas_call(kernel, out_shape=jax.ShapeDtypeStruct(out_shape, bf16), i...  77.5 us
    pallas_call x1, Pallas kernels, late_reduce(): pl.pallas_call(late_kernel, out_shape=(jax.ShapeDtypeStruct((192, 768), f...  47.5 us
    pallas_call x1, Pallas kernels, attend(): pl.pallas_call(functools.partial(attend_kernel, q_rows=512, k_rows=1024),...  43.8 us
    dot_general x9, matrix products, contract(): lax.dot_general(left, right, (((left_dim,), (right_dim,)), ((), ())), pre...  32.6 us
    pallas_call x1, Pallas kernels, first_weights(): pl.pallas_call(first_weights_kernel, out_shape=(jax.ShapeDtypeStruct((4 *...  18.4 us
    dot_general x3, matrix products, dot(): return jnp.dot(left, right, preferred_element_type=f32)  17.3 us

profile of v2, /device:TPU:0, one launch (start us, length us, event | category | flops | bytes accessed | tf_op | source)
XLA Modules:
  0.0 341.6 jit_solution(6023212873647841450)
XLA Ops:
  0.6 0.0 copy-start.25
  0.7 1.3 reshape.225.refs_5_
  2.0 18.4 %first_weights.1 = (bf16[768,2304]{1,0:T(8,128)(2,1)}, bf16[128,768]{1,0:T(8,128)(2,1)}) custom-call(f32[192,2304]{1,0:T(8,128)} %weight.1, f32[1,192]{1,0:T(1,128)} %bitcast.83, f32[1,192]{1,0:T(1,128)} %bitcast.84, f32[1,192]{1,0:T(1,128)} %bitcast.85, f32[1,192]{1,0:T(1,128)} %bitcast.86, f32[1,192]{1,0:T(1,128)} %bitcast.87, f32[1,768]{1,0:T(1,128)} %reshape.225.refs_5_, ...), custom_call_target="tpu_custom_call" | custom-call | tf_op jit(solution)/shard_map/first_weights/pallas_call | solution.py:274
  20.4 1.0 bitcast_convert_fusion.1
  21.3 0.1 slice_reduce_fusion.1
  21.4 0.1 add.130
  21.6 1.2 dynamic_slice.11
  23.5 0.1 fusion.19
  23.6 0.1 reshape_squeeze.7
  23.7 0.1 reshape_squeeze.6
  23.8 4.6 %fusion.1 = bf16[2304,256]{1,0:T(8,128)(2,1)} fusion(bf16[768,2304]{1,0:T(8,128)(2,1)} %get-tuple-element.30, bf16[256,768]{1,0:T(8,128)(2,1)S(1)} %get-tuple-element.74, f32[2304]{0:T(1024)S(1)} %copy-done.25, f32[2304]{0:T(1024)S(1)} %pad_maximum_fusion), kind=kOutput, calls=%fused_computation.7 | convolution fusion | flops 907739136 | bytes 5130240 | tf_op jit(solution)/shard_map/dot_general | solution.py:46
  28.4 26.9 %to_heads.1.x_ref = bf16[32,3,64,128]{3,2,1,0:T(8,128)(2,1)} custom-call(bf16[3,12,64,256]{3,2,1,0:T(8,128)(2,1)} %bitcast.79), custom_call_target="tpu_custom_call" | custom-call | tf_op jit(solution)/shard_map/to_heads/pallas_call | solution.py:160
  55.3 43.8 %attend.1 = (f32[32,64,128]{2,1,0:T(8,128)}, bf16[32,64,128]{2,1,0:T(8,128)(2,1)}, f32[32,8,128]{2,1,0:T(8,128)}, bf16[768,768]{1,0:T(8,128)(2,1)}, bf16[768,307...) custom-call(s32[1]{0:T(128)} %bitcast.2.len_ref, bf16[32,3,64,128]{3,2,1,0:T(8,128)(2,1)} %to_heads.1.x_ref, f32[192,768]{1,0:T(8,128)} %w0.1, ...), custom_call_target="tpu_custom_call" | custom-call | tf_op jit(solution)/shard_map/attend/pallas_call | solution.py:353
  99.0 0.1 add.119
  99.1 17.3 %mixed_to_tokens.1 = bf16[12,64,256]{2,1,0:T(8,128)(2,1)} custom-call(bf16[32,64,128]{2,1,0:T(8,128)(2,1)} %get-tuple-element.32.src), custom_call_target="tpu_custom_call" | custom-call | tf_op jit(solution)/shard_map/mixed_to_tokens/pallas_call | solution.py:160
  116.4 2.0 fusion.22
  118.4 0.1 add.124
  118.4 0.1 mul.165
  118.5 0.2 multiply_reduce_fusion.4
  118.8 11.4 %multiply_convert_fusion = (bf16[256,3072]{1,0:T(8,128)(2,1)S(1)}, f32[256,3072]{1,0:T(8,128)}, f32[256,3072]{1,0:T(8,128)}) fusion(f32[3072]{0:T(1024)S(1)} %bitcast.82, bf16[768,3072]{1,0:T(8,128)(2,1)} %get-tuple-element.34, f32[256,768]{1,0:T(8,128)S(1)} %get-tuple-element.84, f32[768]{0:T(1024)S(1)} %add.124, f32[768]{0:T(1024)S(1)} %mul.165, ...), kind=kOutput, calls=%fused_computation.11 | convolution fusion | flops 1260847104 | bytes 13389824 | tf_op jit(solution)/shard_map/dot_general | solution.py:42
  130.2 4.4 %fusion.23 = (f32[256]{0:T(256)S(1)}, f32[256,768]{1,0:T(8,128)S(1)}) fusion(f32[768]{0:T(1024)S(1)} %add.130, bf16[256,3072]{1,0:T(8,128)(2,1)S(1)} %get-tuple-element.70, bf16[3072,768]{1,0:T(8,128)(2,1)} %get-tuple-element.35, f32[768]{0:T(1024)S(1)} %add.124, f32[768]{0:T(1024)S(1)} %mul.165, f32[256]{0:T(256)S(1)} %fusion.12, ...), kind=kOutput, calls=%fused_computation.83 | convolution fusion | flops 1209335552 | bytes 7876608 | tf_op jit(solution)/shard_map/dot_general | solution.py:42
  134.6 0.2 multiply_reduce_fusion.3
  134.9 0.1 mul.174
  135.0 0.9 fusion.10
  135.8 0.6 multiply_multiply_fusion.6
  136.4 0.7 add.135
  137.1 2.1 fusion.17
  139.2 0.1 convert_reduce_fusion.3
  139.4 6.2 %convert_reduce_fusion = (f32[3072]{0:T(1024)}, bf16[256,3072]{1,0:T(8,128)(2,1)S(1)}) fusion(f32[256,3072]{1,0:T(8,128)S(1)} %copy-done.26, f32[256,3072]{1,0:T(8,128)} %get-tuple-element.85, bf16[256,768]{1,0:T(8,128)(2,1)S(1)} %get-tuple-element.61, bf16[3072,768]{1,0:T(8,128)(2,1)} %get-tuple-element.35), kind=kOutput, calls=%fused_computation.9 | convolution fusion | flops 1220539392 | bytes 12988416 | tf_op jit(solution)/shard_map/dot_general | solution.py:46
  145.7 2.2 multiply_reduce_fusion
  147.9 0.3 fusion.16
  148.3 0.7 convert_reduce_fusion.4
  149.0 0.2 copy-done.9
  149.2 1.2 convolution_convert_fusion.4
  150.4 11.9 %grad_to_heads.1.d_ref = bf16[32,64,128]{2,1,0:T(8,128)(2,1)} custom-call(bf16[12,64,256]{2,1,0:T(8,128)(2,1)} %bitcast.81), custom_call_target="tpu_custom_call" | custom-call | tf_op jit(solution)/shard_map/grad_to_heads/pallas_call | solution.py:160
  162.4 5.2 %convolution_convert_fusion.2 = bf16[768,3072]{1,0:T(8,128)(2,1)} fusion(bf16[256,3072]{1,0:T(8,128)(2,1)} %copy-done.8, f32[256,768]{1,0:T(8,128)S(1)} %get-tuple-element.84, f32[768]{0:T(1024)S(1)} %add.124, f32[768]{0:T(1024)S(1)} %mul.165, f32[256]{0:T(256)} %copy-done.15, f32[256]{0:T(256)S(1)} %broadcast_multiply_fusion.1), kind=kOutput, calls=%fused_computation.2 | convolution fusion | flops 1211301888 | bytes 7086080 | tf_op jit(solution)/shard_map/dot_general | solution.py:46
  167.6 3.6 %convolution_convert_fusion.1 = bf16[3072,768]{1,0:T(8,128)(2,1)} fusion(bf16[256,3072]{1,0:T(8,128)(2,1)S(1)} %copy-done.3, bf16[256,768]{1,0:T(8,128)(2,1)S(1)} %get-tuple-element.61), kind=kOutput, calls=%fused_computation.1 | convolution fusion | flops 1210318848 | bytes 6684672 | tf_op jit(solution)/shard_map/dot_general | solution.py:46
  171.3 0.1 reshape.236
  171.3 0.1 reshape.237
  171.4 0.1 reshape.238
  171.5 0.1 reshape.240
  171.6 0.1 reshape.241
  171.7 0.1 reduce_sum.174
  171.7 0.1 reshape.242
  171.8 0.1 concatenate.10
  171.9 0.6 reshape.243.small_src
  172.6 81.3 %attend_back.1 = (bf16[32,3,64,128]{3,2,1,0:T(8,128)(2,1)}, f32[192,3072]{1,0:T(8,128)}, f32[768,768]{1,0:T(8,128)}, f32[64,128]{1,0:T(8,128)}) custom-call(s32[1]{0:T(128)} %bitcast.2.len_ref, bf16[32,3,64,128]{3,2,1,0:T(8,128)(2,1)} %to_heads.1.x_ref, f32[32,64,128]{2,1,0:T(8,128)} %get-tuple-element.36.o_ref, f32[32,8,128]{2,1,0:T(8,128)} %get-tuple-element.37.lse_ref, ...), custom_call_target="tpu_custom_call" | custom-call | tf_op jit(solution)/shard_map/attend_back/pallas_call | solution.py:768
  253.9 21.4 %grad_to_tokens.1 = bf16[3,12,64,256]{3,2,1,0:T(8,128)(2,1)} custom-call(bf16[32,3,64,128]{3,2,1,0:T(8,128)(2,1)} %get-tuple-element.38.src), custom_call_target="tpu_custom_call" | custom-call | tf_op jit(solution)/shard_map/grad_to_tokens/pallas_call | solution.py:160
  275.4 4.5 %convolution_add_fusion.3 = f32[256,768]{1,0:T(8,128)} fusion(bf16[2304,256]{1,0:T(8,128)(2,1)} %bitcast.72, bf16[768,2304]{1,0:T(8,128)(2,1)} %get-tuple-element.30, f32[256,768]{1,0:T(8,128)S(1)} %get-tuple-element.67, f32[256]{0:T(256)S(1)} %copy-done.24), kind=kOutput, calls=%fused_computation.28 | convolution fusion | flops 906362880 | bytes 6292480 | tf_op jit(solution)/shard_map/dot_general | solution.py:46
  279.9 1.5 convolution_convert_fusion.3
  281.3 2.9 convolution_convert_fusion
  284.3 0.3 convert_reduce_fusion.2
  284.5 0.1 reshape.249
  284.6 0.1 reshape.248
  284.7 0.1 pad_maximum_fusion.1
  284.8 0.6 reshape.250.small_src
  285.4 47.5 %late_reduce.1 = (f32[192,768]{1,0:T(8,128)}, f32[192,2304]{1,0:T(8,128)}, f32[16,128]{1,0:T(8,128)}) custom-call(bf16[2,2,3,4,16,768]{5,4,3,2,1,0:T(8,128)(2,1)} %bitcast.74, bf16[2,2,3,4,16,2304]{5,4,3,2,1,0:T(8,128)(2,1)} %bitcast.70, f32[16,128]{1,0:T(8,128)} %reshape.250.small_src), custom_call_target="tpu_custom_call" | custom-call | tf_op jit(solution)/shard_map/late_reduce/pallas_call | solution.py:815
  332.9 0.9 reshape.251
  333.8 0.7 fusion.20
  334.5 0.7 dynamic-slice_reduce_fusion
  335.1 2.8 copy.35
  337.9 0.8 copy.36
  338.8 1.4 copy.37
  340.2 1.4 copy.38
  (70 shorter events, 0.2 us)
Async XLA Ops:
  0.6 23.1 %copy-start.25 = (f32[2304]{0:T(1024)S(1)}, f32[2304]{0:T(1024)}, u32[]{:S(2)}) copy-start(f32[2304]{0:T(1024)} %constant.111.clone.1) | copy-start | bytes 27652
  0.7 22.8 %copy-start.5 = (f32[2,128,768]{2,1,0:T(8,128)S(1)}, f32[2,128,768]{2,1,0:T(8,128)}, u32[]{:S(2)}) copy-start(f32[2,128,768]{2,1,0:T(8,128)} %param.16) | copy-start | bytes 2359300
  118.8 11.4 %copy-start.18 = (f32[256]{0:T(256)}, f32[256]{0:T(256)S(1)}, u32[]{:S(2)}) copy-start(f32[256]{0:T(256)S(1)} %multiply_reduce_fusion.4) | copy-start | bytes 3076
  118.8 11.4 %copy-start.15 = (f32[256]{0:T(256)}, f32[256]{0:T(256)S(1)}, u32[]{:S(2)}) copy-start(f32[256]{0:T(256)S(1)} %fusion.12) | copy-start | bytes 3076
  130.2 4.4 %copy-start.2 = (bf16[256,3072]{1,0:T(8,128)(2,1)}, bf16[256,3072]{1,0:T(8,128)(2,1)S(1)}, u32[]{:S(2)}) copy-start(bf16[256,3072]{1,0:T(8,128)(2,1)S(1)} %get-tuple-element.70) | copy-start | bytes 4718596
  130.2 4.8 %copy-start.1 = (f32[2,128,768]{2,1,0:T(8,128)S(1)}, f32[2,128,768]{2,1,0:T(8,128)}, u32[]{:S(2)}) copy-start(f32[2,128,768]{2,1,0:T(8,128)} %param.31) | copy-start | bytes 2359300
  134.6 1.8 copy-start.14
  134.9 1.6 copy-start.20
  137.1 2.3 copy-start.26
  139.2 6.4 %slice-start = ((s8[4718592]{0:T(1024)(128)(4,1)}), s8[4194304]{0:T(1024)(128)(4,1)S(1)}, s32[]{:S(2)}) async-start(s8[4718592]{0:T(1024)(128)(4,1)} %bitcast.99), calls=%async_computation | async-start | bytes 8388608
  139.4 6.3 %copy-start.16 = (f32[256]{0:T(256)S(1)}, f32[256]{0:T(256)}, u32[]{:S(2)}) copy-start(f32[256]{0:T(256)} %copy-done.15) | copy-start | bytes 3076
  139.4 6.2 %slice-start.1 = ((s8[4718592]{0:T(1024)(128)(4,1)}), s8[524288]{0:T(1024)(128)(4,1)S(1)}, s32[]{:S(2)}) async-start(s8[4718592]{0:T(1024)(128)(4,1)} %bitcast.99), calls=%async_computation.1 | async-start | bytes 1048576
  145.6 2.3 copy-start.8
  145.6 2.3 copy-start.19
  147.9 1.3 copy-start.9
  148.3 2.1 copy-start.23
  162.4 5.3 %copy-start.3 = (bf16[256,3072]{1,0:T(8,128)(2,1)S(1)}, bf16[256,3072]{1,0:T(8,128)(2,1)}, u32[]{:S(2)}) copy-start(bf16[256,3072]{1,0:T(8,128)(2,1)} %copy-done.2) | copy-start | bytes 4718596
  167.6 3.7 %copy-start.13 = (f32[768]{0:T(1024)S(1)}, f32[768]{0:T(1024)}, u32[]{:S(2)}) copy-start(f32[768]{0:T(1024)} %get-tuple-element.64) | copy-start | bytes 9220
  167.6 3.7 %copy-start.22 = (f32[768]{0:T(1024)S(1)}, f32[768]{0:T(1024)}, u32[]{:S(2)}) copy-start(f32[768]{0:T(1024)} %get-tuple-element.47) | copy-start | bytes 9220
  167.6 3.8 %copy-start.21 = (f32[768]{0:T(1024)S(1)}, f32[768]{0:T(1024)}, u32[]{:S(2)}) copy-start(f32[768]{0:T(1024)} %get-tuple-element.51) | copy-start | bytes 9220
  167.6 3.9 %copy-start.17 = (f32[3072]{0:T(1024)S(1)}, f32[3072]{0:T(1024)}, u32[]{:S(2)}) copy-start(f32[3072]{0:T(1024)} %get-tuple-element.62) | copy-start | bytes 36868
  167.6 4.0 %copy-start.12 = (f32[768]{0:T(1024)S(1)}, f32[768]{0:T(1024)}, u32[]{:S(2)}) copy-start(f32[768]{0:T(1024)} %get-tuple-element.45) | copy-start | bytes 9220
  172.6 102.8 %copy-start.24 = (f32[256]{0:T(256)S(1)}, f32[256]{0:T(256)}, u32[]{:S(2)}) copy-start(f32[256]{0:T(256)} %copy-done.23) | copy-start | bytes 3076
  275.3 4.5 %copy-start.4 = (bf16[12,64,256]{2,1,0:T(8,128)(2,1)S(1)}, bf16[12,64,256]{2,1,0:T(8,128)(2,1)}, u32[]{:S(2)}) copy-start(bf16[12,64,256]{2,1,0:T(8,128)(2,1)} %mixed_to_tokens.1) | copy-start | bytes 1179652
  275.3 6.0 %copy-start = (bf16[3,12,64,256]{3,2,1,0:T(8,128)(2,1)S(1)}, bf16[3,12,64,256]{3,2,1,0:T(8,128)(2,1)}, u32[]{:S(2)}) copy-start(bf16[3,12,64,256]{3,2,1,0:T(8,128)(2,1)} %grad_to_tokens.1) | copy-start | bytes 3538948
  284.2 48.7 %copy-start.11 = (f32[64,128]{1,0:T(8,128)S(1)}, f32[64,128]{1,0:T(8,128)}, u32[]{:S(2)}) copy-start(f32[64,128]{1,0:T(8,128)} %get-tuple-element.42) | copy-start | bytes 98308
  332.9 5.1 %copy-start.10 = (f32[192,768]{1,0:T(8,128)S(1)}, f32[192,768]{1,0:T(8,128)}, u32[]{:S(2)}) copy-start(f32[192,768]{1,0:T(8,128)} %get-tuple-element.111) | copy-start | bytes 1769476
  332.9 5.9 %copy-start.7 = (f32[192,3072]{1,0:T(8,128)S(1)}, f32[192,3072]{1,0:T(8,128)}, u32[]{:S(2)}) copy-start(f32[192,3072]{1,0:T(8,128)} %get-tuple-element.115) | copy-start | bytes 7077892
  337.9 2.2 copy-start.6
